TPU v7x, 256 devices: a whole 4x4x8 slice. The times are simulated.
256 devices in a mesh: hst: 32 (over z, x), tp: 8 (over y, core).
Axes of the slice: x: 4, y: 4, z: 8, core: 2. Of those that a mesh axis runs over, the one named last changes fastest.
Arguments:
- queries: bfloat16 [2048, 4096], P('hst', 'tp')
- key_page_cache: bfloat16 [16384, 16, 1024], P('hst', None, 'tp')
- value_page_cache: bfloat16 [16384, 16, 1024], P('hst', None, 'tp'), may hold values from -5 to 5
- request_pages: int32 [2048, 8], P('hst'), may hold values from 0 to 511, as said below
- context_length: int32 [2048], P('hst'), may hold values from 2 to 128, as said below
- output_weight: bfloat16 [4096, 4096], P('tp'), may hold values from -0.09375 to 0.09375
- adapter_down_weight: bfloat16 [1024, 64, 4096], P('hst', None, 'tp'), may hold values from -0.09375 to 0.09375
- adapter_up_weight: bfloat16 [1024, 64, 4096], P('hst', None, 'tp'), may hold values from -0.75 to 0.75
- residual: bfloat16 [2048, 4096], P('hst', 'tp'), may hold values from -6 to 6
- host_slot_adapter: int32 [1024], P('hst'), may hold values from 0 to 1023, as said below
- request_slot: int32 [2048, 1], P('hst'), may hold values from 0 to 31; in each aligned block of 64 rows (0 to 63, 64 to 127, ...) at most 4 rows name the same one
Outputs:
- hidden_out: bfloat16 [2048, 4096], P('hst', 'tp')
Inputs may be any that keep to these rules, and one draw needn't show every extreme that they name: `request_pages`: entries of one host are its pages 512 in some order: every page of the host belongs to exactly one request. `context_length`: some request of every host has exactly 128 cached tokens. `host_slot_adapter`: A host's 32 entries name different adapters; adapter a is owned by host a // 32. No owner serves more than 2 slots of one host, and some owner serves exactly 2 slots of every host. `request_slot`: at most 4 of the rows of one host name one slot.
All inputs are finite; a program needn't handle non-finite values.
Results may differ from a plain program's by a relative error of at most 0.0085.
Values may be sent and summed in bfloat16 or wider, within the bound.
A program may use at most 128 MiB of HBM per device.

v0:
```python
import math

import jax
import jax.numpy as jnp
from jax import lax
from jax.sharding import PartitionSpec as P

HD = 128


ADAPTER_SCALE = 2.0


def attend_rows(queries, key_page_cache, value_page_cache, request_pages, context_length):
    row_count = queries.shape[0]
    kv_here = key_page_cache.shape[2] // HD
    heads_here = queries.shape[1] // HD
    group_size = heads_here // kv_here
    key_rows = key_page_cache[request_pages].reshape(row_count, -1, kv_here, HD)
    value_rows = value_page_cache[request_pages].reshape(row_count, -1, kv_here, HD)
    query_rows = queries.reshape(row_count, kv_here, group_size, HD)
    query_match_logits = jnp.einsum(
        "rkgd,rtkd->rkgt", query_rows, key_rows, preferred_element_type=jnp.float32
    ) / math.sqrt(HD)
    live_mask = jnp.arange(key_rows.shape[1])[None, :] < context_length[:, None]
    query_match_logits = jnp.where(live_mask[:, None, None, :], query_match_logits, -jnp.inf)
    attn_weights = jax.nn.softmax(query_match_logits, axis=-1).astype(jnp.bfloat16)
    attended = jnp.einsum(
        "rkgt,rtkd->rkgd", attn_weights, value_rows, preferred_element_type=jnp.float32
    )
    return attended.astype(jnp.bfloat16).reshape(row_count, heads_here * HD)


def slot_dispatch(request_slot, slot_total, slot_capacity):
    chosen = request_slot[:, 0]
    row_order = jnp.arange(chosen.shape[0])
    same_slot = chosen[:, None] == chosen[None, :]
    earlier = row_order[None, :] < row_order[:, None]
    before = jnp.sum(same_slot & earlier, axis=1)
    target = chosen * slot_capacity + before
    return jnp.arange(slot_total * slot_capacity)[:, None] == target[None, :]


def owner_slots(host_slot_adapter, owned_total):
    owners = host_slot_adapter // owned_total
    slot_order = jnp.arange(owners.shape[0])
    same_owner = owners[:, None] == owners[None, :]
    before = jnp.sum(same_owner & (slot_order[None, :] < slot_order[:, None]), axis=1)
    return (owners, before)


def local(
    queries,
    key_page_cache,
    value_page_cache,
    request_pages,
    context_length,
    output_weight,
    adapter_down_weight,
    adapter_up_weight,
    residual,
    host_slot_adapter,
    request_slot,
):
    attended = attend_rows(queries, key_page_cache, value_page_cache, request_pages, context_length)
    slot_total = host_slot_adapter.shape[0]
    row_count = attended.shape[0]
    slot_capacity = 2 * row_count // slot_total
    feature_here = attended.shape[1]
    local_output = adapter_up_weight.shape[2]
    owned_total = adapter_up_weight.shape[0]
    host_count = lax.axis_size("hst")
    per_owner = 2 * slot_total // host_count
    dispatch = slot_dispatch(request_slot, slot_total, slot_capacity)
    blocks = jnp.dot(dispatch.astype(jnp.bfloat16), attended, preferred_element_type=jnp.float32)
    blocks = blocks.astype(jnp.bfloat16).reshape(slot_total, slot_capacity, feature_here)
    owners, position = owner_slots(host_slot_adapter, owned_total)
    everyone = lax.all_gather(host_slot_adapter, "hst", axis=0, tiled=True)
    request_table = everyone.reshape(host_count, slot_total)
    owned_here = request_table // owned_total == lax.axis_index("hst")
    slot_order = jnp.arange(slot_total)
    earlier = slot_order[None, :] < slot_order[:, None]
    ahead_count = jnp.sum(owned_here[:, None, :] & earlier[None, :, :], axis=2)
    select_mask = owned_here[:, None, :] & (
        ahead_count[:, None, :] == jnp.arange(per_owner)[None, :, None]
    )
    local_index = request_table % owned_total
    picked_adapters = jnp.sum(jnp.where(select_mask, local_index[:, None, :], 0), axis=2)
    filled_slots = jnp.any(select_mask, axis=2)[:, :, None, None]
    down_outgoing = jnp.where(filled_slots, adapter_down_weight[picked_adapters], 0)
    up_outgoing = jnp.where(filled_slots, adapter_up_weight[picked_adapters], 0)
    got_down, got_up = (
        lax.all_to_all(down_outgoing, "hst", split_axis=0, concat_axis=0, tiled=True),
        lax.all_to_all(up_outgoing, "hst", split_axis=0, concat_axis=0, tiled=True),
    )
    slot_down = got_down[owners, position]
    slot_up_weight = got_up[owners, position]
    partial_sum = jnp.einsum("scd,skd->sck", blocks, slot_down, preferred_element_type=jnp.float32)
    reduced_activations = lax.psum(partial_sum, "tp").astype(jnp.bfloat16)
    adapter_blocks = jnp.einsum(
        "anp,api->ani", reduced_activations, slot_up_weight, preferred_element_type=jnp.float32
    )
    adapter_rows = jnp.dot(
        dispatch.astype(jnp.float32).T,
        adapter_blocks.reshape(slot_total * slot_capacity, local_output),
        precision=lax.Precision.HIGHEST,
    )
    base_terms = jnp.dot(attended, output_weight, preferred_element_type=jnp.float32)
    base_output = lax.psum_scatter(
        base_terms.astype(jnp.bfloat16), "tp", scatter_dimension=1, tiled=True
    ).astype(jnp.float32)
    return (residual.astype(jnp.float32) + base_output + ADAPTER_SCALE * adapter_rows).astype(
        jnp.bfloat16
    )


def solution(mesh):
    in_specs = (
        P("hst", "tp"),
        P("hst", None, "tp"),
        P("hst", None, "tp"),
        P("hst", None),
        P("hst"),
        P("tp", None),
        P("hst", None, "tp"),
        P("hst", None, "tp"),
        P("hst", "tp"),
        P("hst"),
        P("hst", None),
    )
    out_specs = P("hst", "tp")
    return jax.shard_map(local, mesh=mesh, in_specs=in_specs, out_specs=out_specs, check_vma=False)
```

profile of v0, /device:TPU:1, one launch (start us, length us, event | category | flops | bytes accessed | tf_op | source)
XLA Modules:
  0.0 279.1 jit_solution(13034767761248747833)
XLA Ops:
  6.5 0.0 copy-start
  6.5 1.4 dynamic-slice
  8.6 0.9 dynamic-update-slice
  9.5 19.8 %all-reduce = s32[1024]{0:T(1024)S(1)} all-reduce(s32[1024]{0:T(1024)S(1)} %dynamic-update-slice), channel_id=1, replica_groups=mesh['hst'=32,'tp'=8] {'hst'}, use_global_device_ids=true, to_apply=%add | all-reduce | flops 1024 | bytes 8192
  29.3 0.1 reshape.174
  29.4 0.6 convert_reduce_fusion
  30.1 0.1 fusion.18
  30.2 0.1 select_reduce_fusion
  30.3 0.1 copy.17
  30.4 0.1 reshape.194
  30.5 0.0 copy-done
  30.5 2.8 gather_fusion.4
  33.3 4.4 %gather_fusion.2 = bf16[64,64,512]{2,1,0:T(8,128)(2,1)} fusion(bf16[32,64,512]{2,1,0:T(8,128)(2,1)} %param.17, s32[1024]{0:T(1024)S(1)} %pad_clamp_fusion), kind=kCustom, calls=%fused_computation.2 | custom fusion | bytes 8388864 | tf_op jit(solution)/shard_map/gather | solution.py:90
  37.7 0.1 copy.16
  37.8 5.1 %broadcast_select_fusion = (bf16[32,2,64,512]{3,2,1,0:T(8,128)(2,1)}, bf16[32,2,64,512]{3,2,1,0:T(8,128)(2,1)S(1)}) fusion(bf16[32,2,64,512]{3,2,1,0:T(8,128)(2,1)} %bitcast.42, pred[32,2]{1,0:T(8,128)(4,1)S(1)} %copy.16, bf16[32,2,64,512]{3,2,1,0:T(8,128)(2,1)} %bitcast.43), kind=kLoop, calls=%fused_computation.8 | loop fusion | flops 4194304 | bytes 16777280 | tf_op jit(solution)/shard_map/jit(_where)/select_n | solution.py:91
  42.9 93.0 %all_to_all.10 = bf16[32,2,64,512]{3,2,1,0:T(8,128)(2,1)} all-to-all(bf16[32,2,64,512]{3,2,1,0:T(8,128)(2,1)S(1)} %get-tuple-element.6), channel_id=1, replica_groups=mesh['hst'=32,'tp'=8] {'hst'}, dimensions={0} | all-to-all | bytes 8388608 | tf_op jit(solution)/shard_map/all_to_all | solution.py:93
  135.9 0.0 copy-start.3
  135.9 0.0 copy-start.1
  135.9 8.1 %all-to-all-start.1 = ((bf16[32,2,64,512]{3,2,1,0:T(8,128)(2,1)}), bf16[32,2,64,512]{3,2,1,0:T(8,128)(2,1)}, u32[]{:S(2)}, u32[]{:S(2)}) async-start(bf16[32,2,64,512]{3,2,1,0:T(8,128)(2,1)} %get-tuple-element.5), calls=%async_computation.2 | async-start | bytes 8388608 | tf_op jit(solution)/shard_map/all_to_all | solution.py:94
  144.1 0.0 reduce-scatter.2.cloned.1.call-start
  144.1 0.0 copy-done.3
  144.2 0.1 copy.15
  144.2 0.1 reshape.178
  144.3 0.0 copy-done.1
  144.4 4.0 %gather_fusion = bf16[512,16,128]{2,1,0:T(8,128)(2,1)} fusion(bf16[512,16,128]{2,1,0:T(8,128)(2,1)} %param.12, s32[1024]{0:T(1024)S(1)} %pad_clamp_fusion.1), kind=kCustom, calls=%fused_computation | custom fusion | bytes 4196352 | tf_op jit(solution)/shard_map/gather | solution.py:19
  148.4 4.0 %gather_fusion.1 = bf16[512,16,128]{2,1,0:T(8,128)(2,1)} fusion(bf16[512,16,128]{2,1,0:T(8,128)(2,1)} %param.13, s32[1024]{0:T(1024)S(1)} %pad_clamp_fusion.1), kind=kCustom, calls=%fused_computation.1 | custom fusion | bytes 4196352 | tf_op jit(solution)/shard_map/gather | solution.py:20
  152.4 0.0 copy-done.4
  152.4 0.1 iota_compare_fusion.5
  152.5 2.8 fusion.5
  155.2 0.2 fusion.29
  155.5 2.5 convolution_convert_fusion.2
  158.0 3.9 %convolution_convert_fusion = bf16[64,4096]{1,0:T(8,128)(2,1)} fusion(bf16[512,4096]{1,0:T(8,128)(2,1)} %param.16, bf16[8,8,4,128]{3,2,1,0:T(4,128)(2,1)S(1)} %bitcast.46), kind=kOutput, calls=%fused_computation.7 | convolution fusion | flops 268697600 | bytes 4784128 | tf_op jit(solution)/shard_map/dot_general | solution.py:108
  161.9 0.0 reduce-scatter.2.cloned.1.call-update
  161.9 0.0 copy-done.5
  161.9 0.2 convert_reduce_fusion.1
  162.1 0.2 convolution_convert_fusion.1
  162.3 0.0 copy-done.6
  162.3 0.2 convert_reduce_fusion.2
  162.5 4.2 %gather_fusion.3 = bf16[32,64,512]{2,1,0:T(8,128)(2,1)} fusion(bf16[32,2,64,512]{3,2,1,0:T(8,128)(2,1)} %all_to_all.10, s32[32]{0:T(128)S(1)} %fusion.28), kind=kCustom, calls=%fused_computation.3 | custom fusion | bytes 4194560 | tf_op jit(solution)/shard_map/gather | solution.py:96
  166.8 66.8 %all-to-all-done.1 = bf16[32,2,64,512]{3,2,1,0:T(8,128)(2,1)} async-done(((bf16[32,2,64,512]{3,2,1,0:T(8,128)(2,1)}), bf16[32,2,64,512]{3,2,1,0:T(8,128)(2,1)}, u32[]{:S(2)}, u32[]{:S(2)}) %all-to-all-start.1) | async-done | bytes 4194336 | tf_op jit(solution)/shard_map/all_to_all | solution.py:94
  233.6 4.2 %gather_fusion.5 = bf16[32,64,512]{2,1,0:T(8,128)(2,1)} fusion(bf16[32,2,64,512]{3,2,1,0:T(8,128)(2,1)} %all-to-all-done.1, s32[32]{0:T(128)S(1)} %fusion.28), kind=kCustom, calls=%fused_computation.5 | custom fusion | bytes 4194560 | tf_op jit(solution)/shard_map/gather | solution.py:97
  237.8 2.3 fusion.30
  240.1 28.3 %psum.7 = bf16[32,4,64]{2,1,0:T(4,128)(2,1)S(1)} all-reduce(f32[32,4,64]{2,1,0:T(4,128)S(1)} %fusion.30), channel_id=1, replica_groups=mesh['hst'=32,'tp'=8] {'tp'}, use_global_device_ids=true, to_apply=%region_8.9 | all-reduce | flops 8192 | bytes 49152 | tf_op jit(solution)/shard_map/psum | solution.py:99
  268.4 2.0 fusion.31
  270.4 0.1 reshape.175
  270.5 0.0 reduce-scatter.2.cloned.1.call-done
  270.5 0.0 copy-done.2
  270.5 1.7 fusion.6
  (17 shorter events, 0.2 us)
Async XLA Ops:
  6.5 24.0 %copy-start = (bf16[32,64,512]{2,1,0:T(8,128)(2,1)S(1)}, bf16[32,64,512]{2,1,0:T(8,128)(2,1)}, u32[]{:S(2)}) copy-start(bf16[32,64,512]{2,1,0:T(8,128)(2,1)} %param.18) | copy-start | bytes 6291460
  135.9 8.2 %copy-start.3 = (s32[64,8]{0,1:T(8,128)S(1)}, s32[64,8]{0,1:T(8,128)}, u32[]{:S(2)}) copy-start(s32[64,8]{0,1:T(8,128)} %param.14) | copy-start | bytes 6148
  135.9 8.4 %copy-start.1 = (bf16[64,512]{1,0:T(8,128)(2,1)S(1)}, bf16[64,512]{1,0:T(8,128)(2,1)}, u32[]{:S(2)}) copy-start(bf16[64,512]{1,0:T(8,128)(2,1)} %param.11) | copy-start | bytes 196612
  135.9 97.7 %all-to-all-start.1 = ((bf16[32,2,64,512]{3,2,1,0:T(8,128)(2,1)}), bf16[32,2,64,512]{3,2,1,0:T(8,128)(2,1)}, u32[]{:S(2)}, u32[]{:S(2)}) async-start(bf16[32,2,64,512]{3,2,1,0:T(8,128)(2,1)} %get-tuple-element.5), calls=%async_computation.2 | async-start | bytes 8388608 | tf_op jit(solution)/shard_map/all_to_all | solution.py:94
  144.1 126.4 %reduce-scatter.2.cloned.1.call-start = ((), (), s32[]{:S(2)}) async-start(), calls=%async_computation.3 | async-start | bytes 589824 | tf_op jit(solution)/shard_map/reduce_scatter | solution.py:109
  148.4 4.0 %copy-start.4 = (s32[64]{0:T(128)S(1)}, s32[64]{0:T(128)}, u32[]{:S(2)}) copy-start(s32[64]{0:T(128)} %param.15) | copy-start | bytes 772
  158.0 3.9 %copy-start.5 = (s32[64,1]{0,1:T(1,128)S(1)}, s32[64,1]{0,1:T(1,128)}, u32[]{:S(2)}) copy-start(s32[64,1]{0,1:T(1,128)} %param.21) | copy-start | bytes 772
  158.0 4.3 %copy-start.6 = (s32[32]{0:T(128)S(1)}, s32[32]{0:T(128)}, u32[]{:S(2)}) copy-start(s32[32]{0:T(128)} %param.20) | copy-start | bytes 388
  237.8 32.7 %copy-start.2 = (bf16[64,512]{1,0:T(8,128)(2,1)S(1)}, bf16[64,512]{1,0:T(8,128)(2,1)}, u32[]{:S(2)}) copy-start(bf16[64,512]{1,0:T(8,128)(2,1)} %param.19) | copy-start | bytes 196612
Sparse Core Ops, SparseCore 0:
  162.0 37.5 reduce-scatter.1
where the time goes:
time: 280 us; the launch traced here: 279 us
  blocking collectives  141 us (50%)
  waiting for transfers between devices  66.9 us (24%)
  local copies, waits for them, and re-layouts  26.6 us (10%)
  matrix products  15.3 us (5%)
  between operations  14.2 us (5%)
  starting transfers between devices  8.19 us (3%)
  other arithmetic  6.73 us (2%)
    all_to_all x1, blocking collectives, local(): lax.all_to_all(down_outgoing, 'hst', split_axis=0, concat_axis=0, tiled=T...  93 us
    all_to_all x1, waiting for transfers between devices, local(): lax.all_to_all(up_outgoing, 'hst', split_axis=0, concat_axis=0, tiled=True)  66.8 us
    psum x1, blocking collectives, local(): reduced_activations = lax.psum(partial_sum, 'tp').astype(jnp.bfloat16)  28.3 us
    unnamed x1, blocking collectives  19.8 us
    all_to_all x1, starting transfers between devices, local(): lax.all_to_all(up_outgoing, 'hst', split_axis=0, concat_axis=0, tiled=True)  8.14 us
  transfers between devices with their start and end apart: 2, of which 1 were waited for; matrix products, arithmetic and copies ran while one was open for 11% of the time, Pallas kernels for 0%

commit v1 on v0

v1 whole, which is shorter than its diff:
```python
import functools
import math

import jax
import jax.numpy as jnp
from jax import lax
from jax.experimental import pallas as pl
from jax.experimental.pallas import tpu as pltpu
from jax.sharding import PartitionSpec as P

HD = 128
ADAPTER_SCALE = 2.0
MESH = pl.DeviceIdType.MESH
BF = jnp.bfloat16
F32 = jnp.float32
NT = (((1,), (1,)), ((), ()))
NN = (((1,), (0,)), ((), ()))


def dot(a, b, dims=NN):
    return lax.dot_general(a, b, dims, preferred_element_type=F32)


def iota(shape, dim):
    return lax.broadcasted_iota(jnp.int32, shape, dim)


def kernel(
    n_hst,
    n_tp,
    q_hbm,
    k_hbm,
    v_hbm,
    pages_ref,
    length_ref,
    w_hbm,
    down_hbm,
    up_hbm,
    table_ref,
    slot_ref,
    out_ref,
    q_ref,
    k_ref,
    v_ref,
    w_ref,
    down_ref,
    up_ref,
    att_ref,
    table_out,
    tables,
    rows_out,
    rows_in,
    back_out,
    back_in,
    base_out,
    base_in,
    part_out,
    part_in,
    shrunk,
    local_sem,
    table_send,
    table_recv,
    rows_send,
    rows_recv,
    back_send,
    back_recv,
    base_send,
    base_recv,
    part_send,
    part_recv,
    shrunk_send,
    shrunk_recv,
):
    host = lax.axis_index("hst")
    lane = lax.axis_index("tp")

    def load(src, dst, i):
        return pltpu.make_async_copy(src, dst, local_sem.at[i])

    load_q = load(q_hbm, q_ref, 0)
    load_k = load(k_hbm, k_ref, 1)
    load_v = load(v_hbm, v_ref, 2)
    load_w = load(w_hbm, w_ref, 3)
    load_down = load(down_hbm, down_ref, 4)
    load_up = load(up_hbm, up_ref, 5)
    load_q.start()
    load_k.start()
    load_v.start()
    load_w.start()
    load_down.start()
    load_up.start()

    barrier = pltpu.get_barrier_semaphore()

    def greet_hosts(step, carry):
        other = lax.rem(host + step, n_hst)
        pl.semaphore_signal(barrier, inc=1, device_id=(other, lane), device_id_type=MESH)
        return carry

    def greet_lanes(step, carry):
        other = lax.rem(lane + step, n_tp)
        pl.semaphore_signal(barrier, inc=1, device_id=(host, other), device_id_type=MESH)
        return carry

    lax.fori_loop(1, n_hst, greet_hosts, 0)
    lax.fori_loop(1, n_tp, greet_lanes, 0)

    slots = table_ref.shape[1]
    row_total = slot_ref.shape[0]
    table_out[...] = jnp.full(table_out.shape, -1, jnp.int32)
    table_out[0:1, 0:slots] = table_ref[...]
    table_row = table_out[0:1, :]
    owner_row = jnp.right_shift(table_row, 5)
    owner_all = jnp.broadcast_to(owner_row, (128, 128))
    s_sub, s_lane = iota((128, 128), 0), iota((128, 128), 1)
    owner_col = jnp.sum(jnp.where(s_sub == s_lane, owner_all, 0), axis=1, keepdims=True)
    place_row = jnp.sum(
        jnp.where((owner_col == owner_all) & (s_sub < s_lane), 1, 0), axis=0, keepdims=True
    )
    start_row = owner_row * 8 + place_row * 4
    chosen_col = slot_ref[...]
    r_sub, r_lane = iota((row_total, 128), 0), iota((row_total, 128), 1)
    chosen_row = jnp.sum(jnp.where(r_sub == r_lane, chosen_col, 0), axis=0, keepdims=True)
    before_col = jnp.sum(
        jnp.where((chosen_col == chosen_row) & (r_lane < r_sub), 1, 0), axis=1, keepdims=True
    )
    target_col = before_col + jnp.sum(
        jnp.where(chosen_col == r_lane, start_row, 0), axis=1, keepdims=True
    )
    target_row = jnp.sum(jnp.where(r_sub == r_lane, target_col, 0), axis=0, keepdims=True)
    send_total = n_hst * 8
    scatter = jnp.where(
        iota((send_total, row_total), 0) == target_row[:, :row_total], 1.0, 0.0
    ).astype(BF)
    back_place = (target_col // 8) * 16 + lax.rem(target_col, 8)
    back_lane = iota((row_total, n_hst * 16), 1)
    gather_lo = jnp.where(back_lane == back_place, 1.0, 0.0).astype(BF)
    gather_hi = jnp.where(back_lane == back_place + 8, 1.0, 0.0).astype(BF)

    pl.semaphore_wait(barrier, n_hst - 1 + n_tp - 1)

    tables[pl.ds(host, 1), :] = table_row

    def table_copy(other, mine, step):
        return pltpu.make_async_remote_copy(
            src_ref=table_out.at[0:1, :],
            dst_ref=tables.at[pl.ds(mine, 1), :],
            send_sem=table_send.at[step],
            recv_sem=table_recv.at[step],
            device_id=(other, lane),
            device_id_type=MESH,
        )

    def send_table(step, carry):
        table_copy(lax.rem(host + step, n_hst), host, step).start()
        return carry

    lax.fori_loop(1, n_hst, send_table, 0)

    load_q.wait()
    load_k.wait()
    load_v.wait()
    heads = q_ref.shape[1] // HD
    tall = heads * 16
    member = lax.rem(iota((tall, HD), 0), 16)
    token = iota((tall, HD), 1)
    scale = 1.0 / math.sqrt(HD)

    def pages_of(ref, row):
        return [ref[pages_ref[row, p]] for p in range(pages_ref.shape[1])]

    def attend(group, carry):
        first = pl.multiple_of(group * 16, 16)
        q = q_ref[pl.ds(first, 16), :]
        q = jnp.concatenate([q[:, j * HD : (j + 1) * HD] for j in range(heads)], axis=0)
        logits = jnp.full((tall, HD), -jnp.inf, F32)
        for r in range(0, 16, 2):
            keys = jnp.concatenate(pages_of(k_ref, first + r) + pages_of(k_ref, first + r + 1), axis=0)
            s = dot(q, keys, NT)
            for i in range(2):
                live = (member == r + i) & (token < length_ref[first + r + i])
                logits = jnp.where(live, s[:, i * HD : (i + 1) * HD] * scale, logits)
        top = jnp.max(logits, axis=1, keepdims=True)
        e = jnp.exp(logits - top)
        p = e / jnp.sum(e, axis=1, keepdims=True)
        acc = jnp.zeros((tall, HD), F32)
        for r in range(0, 16, 2):
            values = jnp.concatenate(pages_of(v_ref, first + r) + pages_of(v_ref, first + r + 1), axis=0)
            spread = jnp.concatenate([jnp.where(member == r + i, p, 0.0) for i in range(2)], axis=1)
            acc = acc + dot(spread.astype(BF), values)
        acc = acc.astype(BF)
        for j in range(heads):
            att_ref[pl.ds(first, 16), j * HD : (j + 1) * HD] = acc[j * 16 : (j + 1) * 16]
        return carry

    lax.fori_loop(0, row_total // 16, attend, 0)

    att = att_ref[...]
    half = att.shape[1] // 2

    def pack(lo, hi):
        return jnp.concatenate(
            [lo.reshape(n_hst, 8, half), hi.reshape(n_hst, 8, half)], axis=1
        ).astype(BF)

    def unpack(x):
        x = x.astype(F32)
        return (
            x[:, :8].reshape(n_hst * 8, half).astype(BF),
            x[:, 8:].reshape(n_hst * 8, half).astype(BF),
        )

    rows_out[...] = pack(dot(scatter, att[:, :half]), dot(scatter, att[:, half:]))

    def block_copy(out, into, send_sem, recv_sem, other, mine, step):
        return pltpu.make_async_remote_copy(
            src_ref=out.at[other],
            dst_ref=into.at[mine],
            send_sem=send_sem.at[step],
            recv_sem=recv_sem.at[step],
            device_id=(other, lane),
            device_id_type=MESH,
        )

    def send_rows(step, carry):
        block_copy(
            rows_out, rows_in, rows_send, rows_recv, lax.rem(host + step, n_hst), host, step
        ).start()
        return carry

    lax.fori_loop(1, n_hst, send_rows, 0)
    rows_in[pl.ds(host, 1)] = rows_out[pl.ds(host, 1)]

    load_w.wait()
    width = out_ref.shape[1]

    def project(which):
        return dot(att, w_ref[:, pl.ds(pl.multiple_of(which * width, width), width)])

    def base_copy(other, step):
        return pltpu.make_async_remote_copy(
            src_ref=base_out.at[step],
            dst_ref=base_in.at[step],
            send_sem=base_send.at[step],
            recv_sem=base_recv.at[step],
            device_id=(host, other),
            device_id_type=MESH,
        )

    def send_base(step, carry):
        other = lax.rem(lane + step, n_tp)
        base_out[pl.ds(step, 1)] = project(other).astype(BF)[None]
        base_copy(other, step).start()
        return carry

    lax.fori_loop(1, n_tp, send_base, 0)
    own_base = project(lane)

    def wait_table(step, carry):
        table_copy(lax.rem(host + step, n_hst), host, step).wait()
        return carry

    lax.fori_loop(1, n_hst, wait_table, 0)
    table = tables[...]
    owned = jnp.right_shift(table, 5) == host
    ahead = dot(
        jnp.where(owned, 1.0, 0.0).astype(BF), jnp.where(s_sub < s_lane, 1.0, 0.0).astype(BF)
    )
    local_index = jnp.bitwise_and(table, 31).astype(F32)

    def place_index(place):
        got = jnp.where(owned & (ahead == place), local_index, -1.0)
        return jnp.broadcast_to(jnp.max(got, axis=1, keepdims=True), got.shape).astype(BF)

    spread_host = jnp.where(
        iota((send_total, n_hst), 0) // 8 == iota((send_total, n_hst), 1), 1.0, 0.0
    ).astype(BF)
    x_sub, x_lane = iota((send_total, 128), 0), iota((send_total, 128), 1)
    adapter = jnp.where(
        lax.rem(x_sub, 8) < 4,
        dot(spread_host, place_index(0.0)),
        dot(spread_host, place_index(1.0)),
    ) - jnp.where(x_lane >= 64, 1.0, 0.0)

    load_down.wait()

    def wait_rows(step, carry):
        block_copy(
            rows_out, rows_in, rows_send, rows_recv, lax.rem(host + step, n_hst), host, step
        ).wait()
        return carry

    lax.fori_loop(1, n_hst, wait_rows, 0)
    x_lo, x_hi = unpack(rows_in[...])
    owned_total, rank, _ = down_ref.shape
    pairs = owned_total // 2
    folded = jnp.zeros((send_total, 128), F32)
    for c in range(0, pairs, 2):
        d = down_ref[2 * c : 2 * c + 4].reshape(4 * rank, 2 * half)
        s = dot(x_lo, d[:, :half], NT) + dot(x_hi, d[:, half:], NT)
        folded = folded + jnp.where(adapter == 2.0 * c, s[:, :128], 0.0)
        folded = folded + jnp.where(adapter == 2.0 * c + 2.0, s[:, 128:], 0.0)
    folded = folded + pltpu.roll(folded, 64, 1)
    both = send_total // 2
    low_half = iota((both, 128), 1) < 64
    part_out[...] = jnp.where(low_half, folded[:both], folded[both:]).reshape(part_out.shape)

    def part_copy(other, step):
        return pltpu.make_async_remote_copy(
            src_ref=part_out.at[other],
            dst_ref=part_in.at[step],
            send_sem=part_send.at[step],
            recv_sem=part_recv.at[step],
            device_id=(host, other),
            device_id_type=MESH,
        )

    def send_part(step, carry):
        part_copy(lax.rem(lane + step, n_tp), step).start()
        return carry

    lax.fori_loop(1, n_tp, send_part, 0)

    def wait_base(step, carry):
        base_copy(lax.rem(lane + step, n_tp), step).wait()
        return carry

    lax.fori_loop(1, n_tp, wait_base, 0)
    base = own_base
    for step in range(1, n_tp):
        base = base + base_in[step].astype(F32)
    out_ref[...] = base

    def wait_part(step, carry):
        part_copy(lax.rem(lane + step, n_tp), step).wait()
        return carry

    lax.fori_loop(1, n_tp, wait_part, 0)
    total = part_out[lane]
    for step in range(1, n_tp):
        total = total + part_in[step]
    shrunk[pl.ds(lane, 1)] = total.astype(BF)[None]

    def shrunk_copy(other, step):
        return pltpu.make_async_remote_copy(
            src_ref=shrunk.at[lane],
            dst_ref=shrunk.at[lane],
            send_sem=shrunk_send.at[step],
            recv_sem=shrunk_recv.at[step],
            device_id=(host, other),
            device_id_type=MESH,
        )

    def send_shrunk(step, carry):
        shrunk_copy(lax.rem(lane + step, n_tp), step).start()
        return carry

    def wait_shrunk(step, carry):
        shrunk_copy(lax.rem(lane + step, n_tp), step).wait()
        return carry

    lax.fori_loop(1, n_tp, send_shrunk, 0)
    load_up.wait()
    lax.fori_loop(1, n_tp, wait_shrunk, 0)

    g = shrunk[...].reshape(both, 128).astype(F32)
    turned = pltpu.roll(g, 64, 1)
    full = jnp.concatenate(
        [jnp.where(low_half, g, turned), jnp.where(low_half, turned, g)], axis=0
    )
    raised = jnp.zeros((send_total, 2 * half), F32)
    for c in range(0, pairs, 2):
        e = jnp.concatenate(
            [
                jnp.where(adapter == 2.0 * c, full, 0.0),
                jnp.where(adapter == 2.0 * c + 2.0, full, 0.0),
            ],
            axis=1,
        ).astype(BF)
        raised = raised + dot(e, up_ref[2 * c : 2 * c + 4].reshape(4 * rank, 2 * half))
    back_out[...] = pack(raised[:, :half], raised[:, half:])

    def send_back(step, carry):
        block_copy(
            back_out, back_in, back_send, back_recv, lax.rem(host + step, n_hst), host, step
        ).start()
        return carry

    def wait_back(step, carry):
        block_copy(
            back_out, back_in, back_send, back_recv, lax.rem(host + step, n_hst), host, step
        ).wait()
        return carry

    lax.fori_loop(1, n_hst, send_back, 0)
    back_in[pl.ds(host, 1)] = back_out[pl.ds(host, 1)]
    lax.fori_loop(1, n_hst, wait_back, 0)
    y = back_in[...].reshape(n_hst * 16, half)
    out_ref[:, :half] += ADAPTER_SCALE * dot(gather_lo, y)
    out_ref[:, half:] += ADAPTER_SCALE * dot(gather_hi, y)


def local(
    queries,
    key_page_cache,
    value_page_cache,
    request_pages,
    context_length,
    output_weight,
    adapter_down_weight,
    adapter_up_weight,
    residual,
    host_slot_adapter,
    request_slot,
):
    n_hst, n_tp = lax.axis_size("hst"), lax.axis_size("tp")
    rows, width = queries.shape
    any_spec = pl.BlockSpec(memory_space=pl.ANY)
    smem = pl.BlockSpec(memory_space=pltpu.SMEM)
    vmem = pl.BlockSpec(memory_space=pltpu.VMEM)
    dma = pltpu.SemaphoreType.DMA
    block = (n_hst, 16, width // 2)
    part_rows = n_hst * 8 // 2 // n_tp
    summed = pl.pallas_call(
        functools.partial(kernel, n_hst, n_tp),
        out_shape=jax.ShapeDtypeStruct((rows, width), F32),
        in_specs=[any_spec, any_spec, any_spec, smem, smem, any_spec, any_spec, any_spec, vmem, vmem],
        out_specs=vmem,
        scratch_shapes=[
            pltpu.VMEM(queries.shape, BF),
            pltpu.VMEM(key_page_cache.shape, BF),
            pltpu.VMEM(value_page_cache.shape, BF),
            pltpu.VMEM(output_weight.shape, BF),
            pltpu.VMEM(adapter_down_weight.shape, BF),
            pltpu.VMEM(adapter_up_weight.shape, BF),
            pltpu.VMEM(queries.shape, BF),
            pltpu.VMEM((8, 128), jnp.int32),
            pltpu.VMEM((n_hst, 128), jnp.int32),
            pltpu.VMEM(block, BF),
            pltpu.VMEM(block, BF),
            pltpu.VMEM(block, BF),
            pltpu.VMEM(block, BF),
            pltpu.VMEM((n_tp, rows, width), BF),
            pltpu.VMEM((n_tp, rows, width), BF),
            pltpu.VMEM((n_tp, part_rows, 128), F32),
            pltpu.VMEM((n_tp, part_rows, 128), F32),
            pltpu.VMEM((n_tp, part_rows, 128), BF),
            dma((6,)),
            dma((n_hst,)),
            dma((n_hst,)),
            dma((n_hst,)),
            dma((n_hst,)),
            dma((n_hst,)),
            dma((n_hst,)),
            dma((n_tp,)),
            dma((n_tp,)),
            dma((n_tp,)),
            dma((n_tp,)),
            dma((n_tp,)),
            dma((n_tp,)),
        ],
        compiler_params=pltpu.CompilerParams(
            collective_id=0, has_side_effects=True, vmem_limit_bytes=48 * 1024 * 1024
        ),
        cost_estimate=pl.CostEstimate(
            flops=2_000_000_000, bytes_accessed=12_000_000, transcendentals=32768
        ),
        name="decode_step",
    )(
        queries,
        key_page_cache,
        value_page_cache,
        request_pages,
        context_length,
        output_weight,
        adapter_down_weight,
        adapter_up_weight,
        host_slot_adapter.reshape(1, -1),
        request_slot,
    )
    return (residual.astype(F32) + summed).astype(BF)


def solution(mesh):
    in_specs = (
        P("hst", "tp"),
        P("hst", None, "tp"),
        P("hst", None, "tp"),
        P("hst", None),
        P("hst"),
        P("tp", None),
        P("hst", None, "tp"),
        P("hst", None, "tp"),
        P("hst", "tp"),
        P("hst"),
        P("hst", None),
    )
    out_specs = P("hst", "tp")
    return jax.shard_map(local, mesh=mesh, in_specs=in_specs, out_specs=out_specs, check_vma=False)
```

time: 280 us -> 53.9 us (0.19)
  blocking collectives: 141 us -> 0 us
  waiting for transfers between devices: 66.9 us -> 0 us
  Pallas kernels: 0 us -> 46.1 us
  local copies, waits for them, and re-layouts: 26.6 us -> 6.85 us
  matrix products: 15.3 us -> 0 us
  between operations: 14.2 us -> 0.02 us
  starting transfers between devices: 8.19 us -> 0 us
  other arithmetic: 6.73 us -> 0.64 us
    all_to_all x1 -> x0, blocking collectives: 93 us -> none  [local(): lax.all_to_all(down_outgoing, 'hst', split_axis=0, concat_axis=0, tiled=T...]
    all_to_all x1 -> x0, waiting for transfers between devices: 66.8 us -> none  [local(): lax.all_to_all(up_outgoing, 'hst', split_axis=0, concat_axis=0, tiled=True)]
    pallas_call x0 -> x1, Pallas kernels: none -> 46.1 us  [local(): pl.pallas_call(functools.partial(kernel, n_hst, n_tp), out_shape=jax.Shap...]
    psum x1 -> x0, blocking collectives: 28.3 us -> none  [local(): reduced_activations = lax.psum(partial_sum, 'tp').astype(jnp.bfloat16)]
    gather x6 -> x0, local copies, waits for them, and re-layouts: 23.6 us -> none  [the longest x1 4.38 us: local(): adapter_down_weight[picked_adapters]]
    unnamed x1 -> x0, blocking collectives: 19.8 us -> none
    dot_general x7 -> x0, matrix products: 15.3 us -> none  [the longest x1 3.88 us: local(): jnp.dot(attended, output_weight, preferred_element_type=jnp.float32)]
    all_to_all x1 -> x0, starting transfers between devices: 8.14 us -> none  [local(): lax.all_to_all(up_outgoing, 'hst', split_axis=0, concat_axis=0, tiled=True)]
  transfers between devices with their start and end apart: 2 -> 0, of which waited for: 1 -> 0; matrix products, arithmetic and copies ran while one was open for 11% -> 0% of each run, Pallas kernels for 0% -> 0%
where the time goes in v1:
time: 53.9 us; the launch traced here: 53.6 us
  Pallas kernels  46.1 us (86%)
  local copies, waits for them, and re-layouts  6.85 us (13%)
  other arithmetic  0.64 us (1%)
    pallas_call x1, Pallas kernels, local(): pl.pallas_call(functools.partial(kernel, n_hst, n_tp), out_shape=jax.Shap...  46.1 us
    unnamed x14, local copies, waits for them, and re-layouts  6.85 us

profile of v1, /device:TPU:1, one launch (start us, length us, event | category | flops | bytes accessed | tf_op | source)
XLA Modules:
  0.0 53.6 jit_solution(8768077574471607150)
XLA Ops:
  0.0 0.8 %copy.12.pages_ref = s32[64,8]{1,0:T(8,128)S(1)} copy(s32[64,8]{0,1:T(8,128)} %param.14) | data formatting | bytes 4096 | tf_op args[3]
  0.8 0.7 %copy.13.slot_ref = s32[64,1]{1,0:T(8,128)S(1)} copy(s32[64,1]{0,1:T(1,128)} %param.21) | data formatting | bytes 512 | tf_op args[10]
  1.5 0.0 copy-start
  1.5 1.6 %copy-done = bf16[512,16,128]{2,1,0:T(8,128)(2,1)S(1)} copy-done((bf16[512,16,128]{2,1,0:T(8,128)(2,1)S(1)}, bf16[512,16,128]{2,1,0:T(8,128)(2,1)}, u32[]{:S(2)}) %copy-start) | copy-done | bytes 2097176
  3.1 0.0 copy-start.1
  3.1 1.6 %copy-done.1 = bf16[512,16,128]{2,1,0:T(8,128)(2,1)S(1)} copy-done((bf16[512,16,128]{2,1,0:T(8,128)(2,1)S(1)}, bf16[512,16,128]{2,1,0:T(8,128)(2,1)}, u32[]{:S(2)}) %copy-start.1) | copy-done | bytes 2097176
  4.7 0.0 copy-start.2
  4.7 0.8 %copy-done.2 = bf16[64,512]{1,0:T(8,128)(2,1)S(1)} copy-done((bf16[64,512]{1,0:T(8,128)(2,1)S(1)}, bf16[64,512]{1,0:T(8,128)(2,1)}, u32[]{:S(2)}) %copy-start.2) | copy-done | bytes 65560
  5.5 0.0 copy-start.3
  5.5 0.7 %copy-done.3 = s32[64]{0:T(128)S(1)} copy-done((s32[64]{0:T(128)S(1)}, s32[64]{0:T(128)}, u32[]{:S(2)}) %copy-start.3) | copy-done | bytes 280
  6.2 0.0 copy-start.4
  6.2 0.7 %copy-done.4 = s32[32]{0:T(128)S(1)} copy-done((s32[32]{0:T(128)S(1)}, s32[32]{0:T(128)}, u32[]{:S(2)}) %copy-start.4) | copy-done | bytes 152
  6.8 0.0 copy-start.5
  6.9 46.1 %decode_step.1 = f32[64,512]{1,0:T(8,128)S(1)} custom-call(bf16[64,512]{1,0:T(8,128)(2,1)S(1)} %copy-done.2, bf16[512,16,128]{2,1,0:T(8,128)(2,1)S(1)} %copy-done, bf16[512,16,128]{2,1,0:T(8,128)(2,1)S(1)} %copy-done.1, s32[64,8]{1,0:T(8,128)S(1)} %copy.12.pages_ref, s32[64]{0:T(128)S(1)} %copy-done.3, bf16[512,4096]{1,0:T(8,128)(2,1)} %w_hbm.1, ...), custom_call_target="tpu_custom_call" | custom-call | flops 2000000000 | bytes 12000000 | tf_op jit(solution)/shard_map/decode_step/pallas_call | solution.py:424
  53.0 0.0 copy-done.5
  53.0 0.6 %add_convert_fusion = bf16[64,512]{1,0:T(8,128)(2,1)} fusion(f32[64,512]{1,0:T(8,128)S(1)} %decode_step.1, bf16[64,512]{1,0:T(8,128)(2,1)S(1)} %copy-done.5), kind=kLoop, calls=%fused_computation | loop fusion | flops 98304 | bytes 262144 | tf_op jit(solution)/shard_map/convert_element_type | solution.py:481
Async XLA Ops:
  1.5 1.6 %copy-start = (bf16[512,16,128]{2,1,0:T(8,128)(2,1)S(1)}, bf16[512,16,128]{2,1,0:T(8,128)(2,1)}, u32[]{:S(2)}) copy-start(bf16[512,16,128]{2,1,0:T(8,128)(2,1)} %k_hbm.1) | copy-start | bytes 6291460
  3.1 1.6 %copy-start.1 = (bf16[512,16,128]{2,1,0:T(8,128)(2,1)S(1)}, bf16[512,16,128]{2,1,0:T(8,128)(2,1)}, u32[]{:S(2)}) copy-start(bf16[512,16,128]{2,1,0:T(8,128)(2,1)} %v_hbm.1) | copy-start | bytes 6291460
  4.7 0.8 %copy-start.2 = (bf16[64,512]{1,0:T(8,128)(2,1)S(1)}, bf16[64,512]{1,0:T(8,128)(2,1)}, u32[]{:S(2)}) copy-start(bf16[64,512]{1,0:T(8,128)(2,1)} %q_hbm.1) | copy-start | bytes 196612
  5.5 0.7 %copy-start.3 = (s32[64]{0:T(128)S(1)}, s32[64]{0:T(128)}, u32[]{:S(2)}) copy-start(s32[64]{0:T(128)} %length_ref.1) | copy-start | bytes 772
  6.2 0.7 %copy-start.4 = (s32[32]{0:T(128)S(1)}, s32[32]{0:T(128)}, u32[]{:S(2)}) copy-start(s32[32]{0:T(128)} %param.20) | copy-start | bytes 388
  6.8 46.1 %copy-start.5 = (bf16[64,512]{1,0:T(8,128)(2,1)S(1)}, bf16[64,512]{1,0:T(8,128)(2,1)}, u32[]{:S(2)}) copy-start(bf16[64,512]{1,0:T(8,128)(2,1)} %param.19) | copy-start | bytes 196612

commit v2 on v1

v2 whole, which is shorter than its diff:
```python
import functools
import math

import jax
import jax.numpy as jnp
from jax import lax
from jax.experimental import pallas as pl
from jax.experimental.pallas import tpu as pltpu
from jax.sharding import PartitionSpec as P

HD = 128
ADAPTER_SCALE = 2.0
Z, X = 8, 4
GROUPS = 2
MESH = pl.DeviceIdType.MESH
BF = jnp.bfloat16
F32 = jnp.float32
NT = (((1,), (1,)), ((), ()))
NN = (((1,), (0,)), ((), ()))


def dot(a, b, dims=NN):
    return lax.dot_general(a, b, dims, preferred_element_type=F32)


def iota(shape, dim):
    return lax.broadcasted_iota(jnp.int32, shape, dim)


def offsets(step):
    i, j = step // X, lax.rem(step, X)
    dz = Z // 2 + (1 - 2 * lax.rem(i, 2)) * ((i + 1) // 2)
    dx = X // 2 + (1 - 2 * lax.rem(j, 2)) * ((j + 1) // 2)
    return dz, dx


def ahead_of(host, step):
    dz, dx = offsets(step)
    return lax.rem(host // X + dz, Z) * X + lax.rem(lax.rem(host, X) + dx, X)


def behind(host, step):
    dz, dx = offsets(step)
    return lax.rem(host // X + Z - dz, Z) * X + lax.rem(lax.rem(host, X) + X - dx, X)


def kernel(
    n_hst,
    n_tp,
    q_hbm,
    k_hbm,
    v_hbm,
    pages_hbm,
    length_hbm,
    w_hbm,
    down_hbm,
    up_hbm,
    table_hbm,
    slot_hbm,
    out_ref,
    pages_ref,
    length_ref,
    table_ref,
    slot_ref,
    q_ref,
    k_ref,
    v_ref,
    w_ref,
    down_ref,
    up_ref,
    att_ref,
    table_out,
    tables,
    rows_out,
    rows_in,
    back_out,
    back_in,
    base_out,
    base_in,
    part_out,
    part_in,
    local_sem,
    table_send,
    table_recv,
    rows_send,
    rows_recv,
    back_send,
    back_recv,
    base_send,
    base_recv,
    part_send,
    part_recv,
):
    host = lax.axis_index("hst")
    lane = lax.axis_index("tp")

    def load(src, dst, i):
        return pltpu.make_async_copy(src, dst, local_sem.at[i])

    load_table = load(table_hbm, table_ref, 0)
    load_slot = load(slot_hbm, slot_ref, 1)
    load_pages = load(pages_hbm, pages_ref, 2)
    load_length = load(length_hbm, length_ref, 3)
    load_q = load(q_hbm, q_ref, 4)
    load_k = load(k_hbm, k_ref, 5)
    load_v = load(v_hbm, v_ref, 6)
    load_w = load(w_hbm, w_ref, 7)
    load_down = load(down_hbm, down_ref, 8)
    load_up = load(up_hbm, up_ref, 9)
    load_pages.start()
    load_length.start()
    load_table.start()
    load_slot.start()
    load_q.start()
    load_k.start()
    load_v.start()

    barrier = pltpu.get_barrier_semaphore()

    def greet_hosts(step, carry):
        other = ahead_of(host, step)
        pl.semaphore_signal(barrier, inc=1, device_id=(other, lane), device_id_type=MESH)
        return carry

    def greet_lanes(step, carry):
        other = lax.rem(lane + step, n_tp)
        pl.semaphore_signal(barrier, inc=1, device_id=(host, other), device_id_type=MESH)
        return carry

    lax.fori_loop(0, n_hst - 1, greet_hosts, 0)
    lax.fori_loop(1, n_tp, greet_lanes, 0)

    slots = table_ref.shape[1]
    row_total = slot_ref.shape[1]
    load_table.wait()
    load_slot.wait()
    table_out[...] = jnp.full(table_out.shape, -1, jnp.int32)
    table_out[0:1, 0:slots] = table_ref[...]
    table_row = table_out[0:1, :]
    owner_row = jnp.right_shift(table_row, 5)
    owner_all = jnp.broadcast_to(owner_row, (128, 128))
    s_sub, s_lane = iota((128, 128), 0), iota((128, 128), 1)
    owner_col = jnp.sum(jnp.where(s_sub == s_lane, owner_all, 0), axis=1, keepdims=True)
    place_row = jnp.sum(
        jnp.where((owner_col == owner_all) & (s_sub < s_lane), 1, 0), axis=0, keepdims=True
    )
    start_row = owner_row * 8 + place_row * 4
    chosen_row = slot_ref[...]
    r_sub, r_lane = iota((row_total, 128), 0), iota((row_total, 128), 1)
    q_sub, q_lane = iota((row_total, row_total), 0), iota((row_total, row_total), 1)
    chosen_col = jnp.sum(jnp.where(q_sub == q_lane, chosen_row, 0), axis=1, keepdims=True)
    before_col = jnp.sum(
        jnp.where((chosen_col == chosen_row) & (q_lane < q_sub), 1, 0), axis=1, keepdims=True
    )
    target_col = before_col + jnp.sum(
        jnp.where(chosen_col == r_lane, start_row, 0), axis=1, keepdims=True
    )
    target_row = jnp.sum(jnp.where(r_sub == r_lane, target_col, 0), axis=0, keepdims=True)
    send_total = n_hst * 8
    scatter = jnp.where(
        iota((send_total, row_total), 0) == target_row[:, :row_total], 1.0, 0.0
    ).astype(BF)
    back_place = (target_col // 8) * 16 + lax.rem(target_col, 8)
    back_lane = iota((row_total, n_hst * 16), 1)
    gather_lo = jnp.where(back_lane == back_place, 1.0, 0.0).astype(BF)
    gather_hi = jnp.where(back_lane == back_place + 8, 1.0, 0.0).astype(BF)

    load_pages.wait()
    load_length.wait()
    load_q.wait()
    load_k.wait()
    load_w.start()
    load_down.start()
    load_up.start()
    load_v.wait()
    heads = q_ref.shape[1] // HD
    tall = heads * 16
    member = lax.rem(iota((tall, HD), 0), 16)
    token = iota((tall, HD), 1)
    scale = 1.0 / math.sqrt(HD)

    def pages_of(ref, row):
        return [ref[pages_ref[p, row]] for p in range(pages_ref.shape[0])]

    def attend(group, carry):
        first = pl.multiple_of(group * 16, 16)
        q = q_ref[pl.ds(first, 16), :]
        q = jnp.concatenate([q[:, j * HD : (j + 1) * HD] for j in range(heads)], axis=0)
        logits = jnp.full((tall, HD), -jnp.inf, F32)
        for r in range(0, 16, 2):
            keys = jnp.concatenate(pages_of(k_ref, first + r) + pages_of(k_ref, first + r + 1), axis=0)
            s = dot(q, keys, NT)
            for i in range(2):
                live = (member == r + i) & (token < length_ref[first + r + i])
                logits = jnp.where(live, s[:, i * HD : (i + 1) * HD] * scale, logits)
        top = jnp.max(logits, axis=1, keepdims=True)
        e = jnp.exp(logits - top)
        p = e / jnp.sum(e, axis=1, keepdims=True)
        acc = jnp.zeros((tall, HD), F32)
        for r in range(0, 16, 2):
            values = jnp.concatenate(pages_of(v_ref, first + r) + pages_of(v_ref, first + r + 1), axis=0)
            spread = jnp.concatenate([jnp.where(member == r + i, p, 0.0) for i in range(2)], axis=1)
            acc = acc + dot(spread.astype(BF), values)
        acc = acc.astype(BF)
        for j in range(heads):
            att_ref[pl.ds(first, 16), j * HD : (j + 1) * HD] = acc[j * 16 : (j + 1) * 16]
        return carry

    lax.fori_loop(0, row_total // 32, attend, 0)

    pl.semaphore_wait(barrier, n_hst - 1 + n_tp - 1)
    tables[pl.ds(host, 1), :] = table_row

    def table_copy(step):
        return pltpu.make_async_remote_copy(
            src_ref=table_out.at[0:1, :],
            dst_ref=tables.at[pl.ds(host, 1), :],
            send_sem=table_send.at[step],
            recv_sem=table_recv.at[step],
            device_id=(ahead_of(host, step), lane),
            device_id_type=MESH,
        )

    def send_table(step, carry):
        table_copy(step).start()
        return carry

    lax.fori_loop(0, n_hst - 1, send_table, 0)
    lax.fori_loop(row_total // 32, row_total // 16, attend, 0)

    att = att_ref[...]
    half = att.shape[1] // 2

    def pack(lo, hi):
        blocks = lo.shape[0] // 8
        return jnp.concatenate(
            [lo.reshape(blocks, 8, half), hi.reshape(blocks, 8, half)], axis=1
        ).astype(BF)

    def unpack(x):
        rows = x.shape[0] * 8
        x = x.astype(F32)
        return x[:, :8].reshape(rows, half).astype(BF), x[:, 8:].reshape(rows, half).astype(BF)

    rows_out[...] = pack(dot(scatter, att[:, :half]), dot(scatter, att[:, half:]))

    def rows_copy(step):
        other = ahead_of(host, step)
        return pltpu.make_async_remote_copy(
            src_ref=rows_out.at[other],
            dst_ref=rows_in.at[step],
            send_sem=rows_send.at[step],
            recv_sem=rows_recv.at[step],
            device_id=(other, lane),
            device_id_type=MESH,
        )

    def send_rows(step, carry):
        rows_copy(step).start()
        return carry

    lax.fori_loop(0, n_hst - 1, send_rows, 0)
    rows_in[n_hst - 1 : n_hst] = rows_out[pl.ds(host, 1)]

    load_w.wait()
    width = out_ref.shape[1]

    def project(which):
        return dot(att, w_ref[:, pl.ds(pl.multiple_of(which * width, width), width)])

    def base_copy(step):
        return pltpu.make_async_remote_copy(
            src_ref=base_out.at[step],
            dst_ref=base_in.at[step],
            send_sem=base_send.at[step],
            recv_sem=base_recv.at[step],
            device_id=(host, lax.rem(lane + step, n_tp)),
            device_id_type=MESH,
        )

    def send_base(step, carry):
        base_out[pl.ds(step, 1)] = project(lax.rem(lane + step, n_tp)).astype(BF)[None]
        base_copy(step).start()
        return carry

    lax.fori_loop(1, n_tp, send_base, 0)
    out_ref[...] = project(lane)

    def wait_table(step, carry):
        table_copy(step).wait()
        return carry

    lax.fori_loop(0, n_hst - 1, wait_table, 0)
    table = tables[...]
    owned = jnp.right_shift(table, 5) == host
    ahead = dot(
        jnp.where(owned, 1.0, 0.0).astype(BF), jnp.where(s_sub < s_lane, 1.0, 0.0).astype(BF)
    )
    local_index = jnp.bitwise_and(table, 31).astype(F32)

    def place_index(place):
        got = jnp.where(owned & (ahead == place), local_index, -1.0)
        return jnp.broadcast_to(jnp.max(got, axis=1, keepdims=True), got.shape).astype(BF)

    group_hosts = n_hst // GROUPS
    group_rows = group_hosts * 8
    place_sub, place_lane = iota((group_rows, 128), 0), iota((group_rows, 128), 1)

    def adapters(group):
        step = group * group_hosts + iota((group_rows, n_hst), 0) // 8
        from_host = jnp.where(behind(host, step) == iota((group_rows, n_hst), 1), 1.0, 0.0).astype(BF)
        return jnp.where(
            lax.rem(place_sub, 8) < 4,
            dot(from_host, place_index(0.0)),
            dot(from_host, place_index(1.0)),
        ) - jnp.where(place_lane >= 64, 1.0, 0.0)

    adapter = [adapters(group) for group in range(GROUPS)]

    owned_total, rank, _ = down_ref.shape
    both = group_rows // 2
    low_half = iota((both, 128), 1) < 64

    def wait_rows(step, carry):
        rows_copy(step).wait()
        return carry

    def part_copy(group, step):
        return pltpu.make_async_remote_copy(
            src_ref=part_out.at[group],
            dst_ref=part_in.at[group * n_tp + step],
            send_sem=part_send.at[group * n_tp + step],
            recv_sem=part_recv.at[group * n_tp + step],
            device_id=(host, lax.rem(lane + step, n_tp)),
            device_id_type=MESH,
        )

    load_down.wait()
    own_part = []
    for group in range(GROUPS):
        first = group * group_hosts
        lax.fori_loop(first, min(first + group_hosts, n_hst - 1), wait_rows, 0)
        x_lo, x_hi = unpack(rows_in[first : first + group_hosts])
        folded = jnp.zeros((group_rows, 128), F32)
        for c in range(0, owned_total, 4):
            d = down_ref[c : c + 4].reshape(4 * rank, 2 * half)
            s = dot(x_lo, d[:, :half], NT) + dot(x_hi, d[:, half:], NT)
            folded = folded + jnp.where(adapter[group] == float(c), s[:, :128], 0.0)
            folded = folded + jnp.where(adapter[group] == float(c + 2), s[:, 128:], 0.0)
        folded = folded + pltpu.roll(folded, 64, 1)
        part = jnp.where(low_half, folded[:both], folded[both:])
        own_part.append(part)
        part_out[group] = part.astype(BF)

        def send_part(step, carry, group=group):
            part_copy(group, step).start()
            return carry

        lax.fori_loop(1, n_tp, send_part, 0)

    def wait_base(step, carry):
        base_copy(step).wait()
        return carry

    lax.fori_loop(1, n_tp, wait_base, 0)
    base = out_ref[...]
    for step in range(1, n_tp):
        base = base + base_in[step].astype(F32)
    out_ref[...] = base

    def back_copy(step):
        other = behind(host, step)
        return pltpu.make_async_remote_copy(
            src_ref=back_out.at[step],
            dst_ref=back_in.at[host],
            send_sem=back_send.at[step],
            recv_sem=back_recv.at[step],
            device_id=(other, lane),
            device_id_type=MESH,
        )

    def send_back(step, carry):
        back_copy(step).start()
        return carry

    def wait_back(step, carry):
        back_copy(step).wait()
        return carry

    load_up.wait()
    for group in range(GROUPS):

        def wait_part(step, carry, group=group):
            part_copy(group, step).wait()
            return carry

        lax.fori_loop(1, n_tp, wait_part, 0)
        g = own_part[group]
        for step in range(1, n_tp):
            g = g + part_in[group * n_tp + step].astype(F32)
        turned = pltpu.roll(g, 64, 1)
        full = jnp.concatenate(
            [jnp.where(low_half, g, turned), jnp.where(low_half, turned, g)], axis=0
        )
        raised = jnp.zeros((group_rows, 2 * half), F32)
        for c in range(0, owned_total, 4):
            e = jnp.concatenate(
                [
                    jnp.where(adapter[group] == float(c), full, 0.0),
                    jnp.where(adapter[group] == float(c + 2), full, 0.0),
                ],
                axis=1,
            ).astype(BF)
            raised = raised + dot(e, up_ref[c : c + 4].reshape(4 * rank, 2 * half))
        first = group * group_hosts
        back_out[first : first + group_hosts] = pack(raised[:, :half], raised[:, half:])
        lax.fori_loop(first, min(first + group_hosts, n_hst - 1), send_back, 0)

    back_in[pl.ds(host, 1)] = back_out[n_hst - 1 : n_hst]
    lax.fori_loop(0, n_hst - 1, wait_back, 0)
    y = back_in[...].reshape(n_hst * 16, half)
    out_ref[:, :half] += ADAPTER_SCALE * dot(gather_lo, y)
    out_ref[:, half:] += ADAPTER_SCALE * dot(gather_hi, y)


def local(
    queries,
    key_page_cache,
    value_page_cache,
    request_pages,
    context_length,
    output_weight,
    adapter_down_weight,
    adapter_up_weight,
    residual,
    host_slot_adapter,
    request_slot,
):
    n_hst, n_tp = lax.axis_size("hst"), lax.axis_size("tp")
    rows, width = queries.shape
    any_spec = pl.BlockSpec(memory_space=pl.ANY)
    dma = pltpu.SemaphoreType.DMA
    block = (n_hst, 16, width // 2)
    part_rows = n_hst * 8 // GROUPS // 2
    arguments = (
        queries,
        key_page_cache,
        value_page_cache,
        request_pages.T,
        context_length,
        output_weight,
        adapter_down_weight,
        adapter_up_weight,
        host_slot_adapter.reshape(1, -1),
        request_slot.T,
    )
    summed = pl.pallas_call(
        functools.partial(kernel, n_hst, n_tp),
        out_shape=jax.ShapeDtypeStruct((rows, width), F32),
        in_specs=[any_spec] * len(arguments),
        out_specs=pl.BlockSpec(memory_space=pltpu.VMEM),
        scratch_shapes=[
            pltpu.SMEM(request_pages.shape[::-1], jnp.int32),
            pltpu.SMEM(context_length.shape, jnp.int32),
            pltpu.VMEM((1, host_slot_adapter.shape[0]), jnp.int32),
            pltpu.VMEM((1, rows), jnp.int32),
            pltpu.VMEM(queries.shape, BF),
            pltpu.VMEM(key_page_cache.shape, BF),
            pltpu.VMEM(value_page_cache.shape, BF),
            pltpu.VMEM(output_weight.shape, BF),
            pltpu.VMEM(adapter_down_weight.shape, BF),
            pltpu.VMEM(adapter_up_weight.shape, BF),
            pltpu.VMEM(queries.shape, BF),
            pltpu.VMEM((8, 128), jnp.int32),
            pltpu.VMEM((n_hst, 128), jnp.int32),
            pltpu.VMEM(block, BF),
            pltpu.VMEM(block, BF),
            pltpu.VMEM(block, BF),
            pltpu.VMEM(block, BF),
            pltpu.VMEM((n_tp, rows, width), BF),
            pltpu.VMEM((n_tp, rows, width), BF),
            pltpu.VMEM((GROUPS, part_rows, 128), BF),
            pltpu.VMEM((GROUPS * n_tp, part_rows, 128), BF),
            dma((10,)),
            dma((n_hst,)),
            dma((n_hst,)),
            dma((n_hst,)),
            dma((n_hst,)),
            dma((n_hst,)),
            dma((n_hst,)),
            dma((n_tp,)),
            dma((n_tp,)),
            dma((GROUPS * n_tp,)),
            dma((GROUPS * n_tp,)),
        ],
        compiler_params=pltpu.CompilerParams(
            collective_id=0, has_side_effects=True, vmem_limit_bytes=40 * 1024 * 1024
        ),
        cost_estimate=pl.CostEstimate(
            flops=2_000_000_000, bytes_accessed=12_000_000, transcendentals=32768
        ),
        name="decode_step",
    )(*(pltpu.with_memory_space_constraint(a, pltpu.HBM) for a in arguments))
    return (residual.astype(F32) + summed).astype(BF)


def solution(mesh):
    in_specs = (
        P("hst", "tp"),
        P("hst", None, "tp"),
        P("hst", None, "tp"),
        P("hst", None),
        P("hst"),
        P("tp", None),
        P("hst", None, "tp"),
        P("hst", None, "tp"),
        P("hst", "tp"),
        P("hst"),
        P("hst", None),
    )
    out_specs = P("hst", "tp")
    return jax.shard_map(local, mesh=mesh, in_specs=in_specs, out_specs=out_specs, check_vma=False)
```

time: 53.9 us -> 40.1 us (0.74)
  local copies, waits for them, and re-layouts: 6.85 us -> 0.01 us
  Pallas kernels: 46.1 us -> 39.3 us
    unnamed x14 -> x2, local copies, waits for them, and re-layouts: 6.85 us -> 0.01 us
    pallas_call x1, Pallas kernels: 46.1 us -> 39.3 us  [local(): pl.pallas_call(functools.partial(kernel, n_hst, n_tp), out_shape=jax.Shap...]
where the time goes in v2:
time: 40.1 us; the launch traced here: 40 us
  Pallas kernels  39.3 us (98%)
  other arithmetic  0.64 us (2%)
    pallas_call x1, Pallas kernels, local(): pl.pallas_call(functools.partial(kernel, n_hst, n_tp), out_shape=jax.Shap...  39.3 us

profile of v2, /device:TPU:1, one launch (start us, length us, event | category | flops | bytes accessed | tf_op | source)
XLA Modules:
  0.0 40.0 jit_solution(13800110595767844779)
XLA Ops:
  0.0 0.0 copy-start
  0.0 39.3 %decode_step.1 = f32[64,512]{1,0:T(8,128)S(1)} custom-call(bf16[64,512]{1,0:T(8,128)(2,1)} %q_hbm.1, bf16[512,16,128]{2,1,0:T(8,128)(2,1)} %k_hbm.1, bf16[512,16,128]{2,1,0:T(8,128)(2,1)} %v_hbm.1, s32[8,64]{1,0:T(8,128)} %bitcast.3, s32[64]{0:T(128)} %length_hbm.1, bf16[512,4096]{1,0:T(8,128)(2,1)} %w_hbm.1, bf16[32,64,512]{2,1,0:T(8,128)(2,1)} %down_hbm.1, ...), custom_call_target="tpu_custom_call" | custom-call | flops 2000000000 | bytes 12000000 | tf_op jit(solution)/shard_map/decode_step/pallas_call | solution.py:457
  39.3 0.0 copy-done
  39.3 0.6 %add_convert_fusion = bf16[64,512]{1,0:T(8,128)(2,1)} fusion(f32[64,512]{1,0:T(8,128)S(1)} %decode_step.1, bf16[64,512]{1,0:T(8,128)(2,1)S(1)} %copy-done), kind=kLoop, calls=%fused_computation | loop fusion | flops 98304 | bytes 262144 | tf_op jit(solution)/shard_map/convert_element_type | solution.py:504
Async XLA Ops:
  0.0 39.3 %copy-start = (bf16[64,512]{1,0:T(8,128)(2,1)S(1)}, bf16[64,512]{1,0:T(8,128)(2,1)}, u32[]{:S(2)}) copy-start(bf16[64,512]{1,0:T(8,128)(2,1)} %param.19) | copy-start | bytes 196612

commit v3 on v2

--- a/solution.py
+++ b/solution.py
@@ -75,6 +75,9 @@
     rows_in,
     back_out,
     back_in,
+    pair_out,
+    pair_in,
+    base_own,
     base_out,
     base_in,
     part_out,
@@ -86,6 +89,8 @@
     rows_recv,
     back_send,
     back_recv,
+    pair_send,
+    pair_recv,
     base_send,
     base_recv,
     part_send,
@@ -108,11 +113,11 @@
     load_down = load(down_hbm, down_ref, 8)
     load_up = load(up_hbm, up_ref, 9)
     load_pages.start()
+    load_q.start()
+    load_k.start()
     load_length.start()
     load_table.start()
     load_slot.start()
-    load_q.start()
-    load_k.start()
     load_v.start()
 
     barrier = pltpu.get_barrier_semaphore()
@@ -206,27 +211,7 @@
             att_ref[pl.ds(first, 16), j * HD : (j + 1) * HD] = acc[j * 16 : (j + 1) * 16]
         return carry
 
-    lax.fori_loop(0, row_total // 32, attend, 0)
-
-    pl.semaphore_wait(barrier, n_hst - 1 + n_tp - 1)
-    tables[pl.ds(host, 1), :] = table_row
-
-    def table_copy(step):
-        return pltpu.make_async_remote_copy(
-            src_ref=table_out.at[0:1, :],
-            dst_ref=tables.at[pl.ds(host, 1), :],
-            send_sem=table_send.at[step],
-            recv_sem=table_recv.at[step],
-            device_id=(ahead_of(host, step), lane),
-            device_id_type=MESH,
-        )
-
-    def send_table(step, carry):
-        table_copy(step).start()
-        return carry
-
-    lax.fori_loop(0, n_hst - 1, send_table, 0)
-    lax.fori_loop(row_total // 32, row_total // 16, attend, 0)
+    lax.fori_loop(0, row_total // 16, attend, 0)
 
     att = att_ref[...]
     half = att.shape[1] // 2
@@ -244,53 +229,90 @@
 
     rows_out[...] = pack(dot(scatter, att[:, :half]), dot(scatter, att[:, half:]))
 
-    def rows_copy(step):
+    def arrived(ref, sem):
+        pltpu.make_async_copy(ref, ref, sem).wait()
+
+    def table_copy(step):
+        return pltpu.make_async_remote_copy(
+            src_ref=table_out.at[0:1, :],
+            dst_ref=tables.at[pl.ds(host, 1), :],
+            send_sem=table_send,
+            recv_sem=table_recv,
+            device_id=(ahead_of(host, step), lane),
+            device_id_type=MESH,
+        )
+
+    def rows_copy(step, group):
         other = ahead_of(host, step)
         return pltpu.make_async_remote_copy(
             src_ref=rows_out.at[other],
             dst_ref=rows_in.at[step],
-            send_sem=rows_send.at[step],
-            recv_sem=rows_recv.at[step],
+            send_sem=rows_send,
+            recv_sem=rows_recv.at[group],
             device_id=(other, lane),
             device_id_type=MESH,
         )
 
-    def send_rows(step, carry):
-        rows_copy(step).start()
-        return carry
-
-    lax.fori_loop(0, n_hst - 1, send_rows, 0)
-    rows_in[n_hst - 1 : n_hst] = rows_out[pl.ds(host, 1)]
+    group_hosts = n_hst // GROUPS
+    last = n_hst - 1
+
+    pl.semaphore_wait(barrier, n_hst - 1 + n_tp - 1)
+    for group in range(GROUPS):
+
+        def send_rows(step, carry, group=group):
+            table_copy(step).start()
+            rows_copy(step, group).start()
+            return carry
+
+        first = group * group_hosts
+        lax.fori_loop(first, min(first + group_hosts, last), send_rows, 0)
+    pltpu.make_async_copy(table_out.at[0:1, :], tables.at[pl.ds(host, 1), :], table_recv).start()
+    pltpu.make_async_copy(rows_out.at[host], rows_in.at[last], rows_recv.at[GROUPS - 1]).start()
 
     load_w.wait()
     width = out_ref.shape[1]
+    chips = n_tp // 2
+    chip, core = lane // 2, lax.rem(lane, 2)
+    turns = (2, 1, 3, 0)
 
     def project(which):
         return dot(att, w_ref[:, pl.ds(pl.multiple_of(which * width, width), width)])
 
-    def base_copy(step):
+    def chip_at(turn):
+        return lax.rem(chip + turn, chips)
+
+    def pair_copy():
         return pltpu.make_async_remote_copy(
-            src_ref=base_out.at[step],
-            dst_ref=base_in.at[step],
-            send_sem=base_send.at[step],
-            recv_sem=base_recv.at[step],
-            device_id=(host, lax.rem(lane + step, n_tp)),
+            src_ref=pair_out,
+            dst_ref=pair_in,
+            send_sem=pair_send,
+            recv_sem=pair_recv,
+            device_id=(host, lane + 1 - 2 * core),
             device_id_type=MESH,
         )
 
-    def send_base(step, carry):
-        base_out[pl.ds(step, 1)] = project(lax.rem(lane + step, n_tp)).astype(BF)[None]
-        base_copy(step).start()
-        return carry
-
-    lax.fori_loop(1, n_tp, send_base, 0)
-    out_ref[...] = project(lane)
-
-    def wait_table(step, carry):
-        table_copy(step).wait()
-        return carry
-
-    lax.fori_loop(0, n_hst - 1, wait_table, 0)
+    def base_copy(i):
+        return pltpu.make_async_remote_copy(
+            src_ref=base_out.at[i],
+            dst_ref=base_in.at[i],
+            send_sem=base_send,
+            recv_sem=base_recv,
+            device_id=(host, 2 * chip_at(turns[i]) + core),
+            device_id_type=MESH,
+        )
+
+    for i, turn in enumerate(turns):
+        pair_out[i] = project(2 * chip_at(turn) + 1 - core).astype(BF)
+    pair_copy().start()
+    for i, turn in enumerate(turns):
+        base_own[i] = project(2 * chip_at(turn) + core)
+    pair_copy().wait()
+    for i in range(chips - 1):
+        base_out[i] = (base_own[i] + pair_in[i].astype(F32)).astype(BF)
+        base_copy(i).start()
+    out_ref[...] = base_own[chips - 1] + pair_in[chips - 1].astype(F32)
+
+    arrived(tables, table_recv)
     table = tables[...]
     owned = jnp.right_shift(table, 5) == host
     ahead = dot(
@@ -302,7 +324,6 @@
         got = jnp.where(owned & (ahead == place), local_index, -1.0)
         return jnp.broadcast_to(jnp.max(got, axis=1, keepdims=True), got.shape).astype(BF)
 
-    group_hosts = n_hst // GROUPS
     group_rows = group_hosts * 8
     place_sub, place_lane = iota((group_rows, 128), 0), iota((group_rows, 128), 1)
 
@@ -321,16 +342,12 @@
     both = group_rows // 2
     low_half = iota((both, 128), 1) < 64
 
-    def wait_rows(step, carry):
-        rows_copy(step).wait()
-        return carry
-
     def part_copy(group, step):
         return pltpu.make_async_remote_copy(
             src_ref=part_out.at[group],
-            dst_ref=part_in.at[group * n_tp + step],
-            send_sem=part_send.at[group * n_tp + step],
-            recv_sem=part_recv.at[group * n_tp + step],
+            dst_ref=part_in.at[group, step - 1],
+            send_sem=part_send,
+            recv_sem=part_recv.at[group],
             device_id=(host, lax.rem(lane + step, n_tp)),
             device_id_type=MESH,
         )
@@ -339,7 +356,7 @@
     own_part = []
     for group in range(GROUPS):
         first = group * group_hosts
-        lax.fori_loop(first, min(first + group_hosts, n_hst - 1), wait_rows, 0)
+        arrived(rows_in.at[first : first + group_hosts], rows_recv.at[group])
         x_lo, x_hi = unpack(rows_in[first : first + group_hosts])
         folded = jnp.zeros((group_rows, 128), F32)
         for c in range(0, owned_total, 4):
@@ -358,14 +375,10 @@
 
         lax.fori_loop(1, n_tp, send_part, 0)
 
-    def wait_base(step, carry):
-        base_copy(step).wait()
-        return carry
-
-    lax.fori_loop(1, n_tp, wait_base, 0)
+    arrived(base_in, base_recv)
     base = out_ref[...]
-    for step in range(1, n_tp):
-        base = base + base_in[step].astype(F32)
+    for i in range(chips - 1):
+        base = base + base_in[i].astype(F32)
     out_ref[...] = base
 
     def back_copy(step):
@@ -373,8 +386,8 @@
         return pltpu.make_async_remote_copy(
             src_ref=back_out.at[step],
             dst_ref=back_in.at[host],
-            send_sem=back_send.at[step],
-            recv_sem=back_recv.at[step],
+            send_sem=back_send,
+            recv_sem=back_recv,
             device_id=(other, lane),
             device_id_type=MESH,
         )
@@ -383,21 +396,12 @@
         back_copy(step).start()
         return carry
 
-    def wait_back(step, carry):
-        back_copy(step).wait()
-        return carry
-
     load_up.wait()
     for group in range(GROUPS):
-
-        def wait_part(step, carry, group=group):
-            part_copy(group, step).wait()
-            return carry
-
-        lax.fori_loop(1, n_tp, wait_part, 0)
+        arrived(part_in.at[group], part_recv.at[group])
         g = own_part[group]
         for step in range(1, n_tp):
-            g = g + part_in[group * n_tp + step].astype(F32)
+            g = g + part_in[group, step - 1].astype(F32)
         turned = pltpu.roll(g, 64, 1)
         full = jnp.concatenate(
             [jnp.where(low_half, g, turned), jnp.where(low_half, turned, g)], axis=0
@@ -414,13 +418,19 @@
             raised = raised + dot(e, up_ref[c : c + 4].reshape(4 * rank, 2 * half))
         first = group * group_hosts
         back_out[first : first + group_hosts] = pack(raised[:, :half], raised[:, half:])
-        lax.fori_loop(first, min(first + group_hosts, n_hst - 1), send_back, 0)
-
-    back_in[pl.ds(host, 1)] = back_out[n_hst - 1 : n_hst]
-    lax.fori_loop(0, n_hst - 1, wait_back, 0)
+        lax.fori_loop(first, min(first + group_hosts, last), send_back, 0)
+
+    pltpu.make_async_copy(back_out.at[last], back_in.at[host], back_recv).start()
+    arrived(back_in, back_recv)
     y = back_in[...].reshape(n_hst * 16, half)
     out_ref[:, :half] += ADAPTER_SCALE * dot(gather_lo, y)
     out_ref[:, half:] += ADAPTER_SCALE * dot(gather_hi, y)
+
+    arrived(tables.at[0:last], table_send)
+    arrived(rows_out.at[0:last], rows_send)
+    arrived(back_out.at[0:last], back_send)
+    arrived(base_out, base_send)
+    arrived(part_in, part_send)
 
 
 def local(
@@ -477,21 +487,26 @@
             pltpu.VMEM(block, BF),
             pltpu.VMEM(block, BF),
             pltpu.VMEM(block, BF),
-            pltpu.VMEM((n_tp, rows, width), BF),
-            pltpu.VMEM((n_tp, rows, width), BF),
+            pltpu.VMEM((n_tp // 2, rows, width), BF),
+            pltpu.VMEM((n_tp // 2, rows, width), BF),
+            pltpu.VMEM((n_tp // 2, rows, width), F32),
+            pltpu.VMEM((n_tp // 2 - 1, rows, width), BF),
+            pltpu.VMEM((n_tp // 2 - 1, rows, width), BF),
             pltpu.VMEM((GROUPS, part_rows, 128), BF),
-            pltpu.VMEM((GROUPS * n_tp, part_rows, 128), BF),
+            pltpu.VMEM((GROUPS, n_tp - 1, part_rows, 128), BF),
             dma((10,)),
-            dma((n_hst,)),
-            dma((n_hst,)),
-            dma((n_hst,)),
-            dma((n_hst,)),
-            dma((n_hst,)),
-            dma((n_hst,)),
-            dma((n_tp,)),
-            dma((n_tp,)),
-            dma((GROUPS * n_tp,)),
-            dma((GROUPS * n_tp,)),
+            dma,
+            dma,
+            dma,
+            dma((GROUPS,)),
+            dma,
+            dma,
+            dma,
+            dma,
+            dma,
+            dma,
+            dma,
+            dma((GROUPS,)),
         ],
         compiler_params=pltpu.CompilerParams(
             collective_id=0, has_side_effects=True, vmem_limit_bytes=40 * 1024 * 1024

time: 40.1 us -> 37.2 us (0.928)
  Pallas kernels: 39.3 us -> 36.5 us
    pallas_call x1, Pallas kernels: 39.3 us -> 36.5 us  [local(): pl.pallas_call(functools.partial(kernel, n_hst, n_tp), out_shape=jax.Shap...]
where the time goes in v3:
time: 37.2 us; the launch traced here: 37.1 us
  Pallas kernels  36.5 us (98%)
  other arithmetic  0.64 us (2%)
    pallas_call x1, Pallas kernels, local(): pl.pallas_call(functools.partial(kernel, n_hst, n_tp), out_shape=jax.Shap...  36.5 us

profile of v3, /device:TPU:1, one launch (start us, length us, event | category | flops | bytes accessed | tf_op | source)
XLA Modules:
  0.0 37.1 jit_solution(7332415701529991697)
XLA Ops:
  0.0 0.0 copy-start
  0.0 36.5 %decode_step.1 = f32[64,512]{1,0:T(8,128)S(1)} custom-call(bf16[64,512]{1,0:T(8,128)(2,1)} %q_hbm.1, bf16[512,16,128]{2,1,0:T(8,128)(2,1)} %k_hbm.1, bf16[512,16,128]{2,1,0:T(8,128)(2,1)} %v_hbm.1, s32[8,64]{1,0:T(8,128)} %bitcast.3, s32[64]{0:T(128)} %length_hbm.1, bf16[512,4096]{1,0:T(8,128)(2,1)} %w_hbm.1, bf16[32,64,512]{2,1,0:T(8,128)(2,1)} %down_hbm.1, ...), custom_call_target="tpu_custom_call" | custom-call | flops 2000000000 | bytes 12000000 | tf_op jit(solution)/shard_map/decode_step/pallas_call | solution.py:467
  36.5 0.0 copy-done
  36.5 0.6 %add_convert_fusion = bf16[64,512]{1,0:T(8,128)(2,1)} fusion(f32[64,512]{1,0:T(8,128)S(1)} %decode_step.1, bf16[64,512]{1,0:T(8,128)(2,1)S(1)} %copy-done), kind=kLoop, calls=%fused_computation | loop fusion | flops 98304 | bytes 262144 | tf_op jit(solution)/shard_map/convert_element_type | solution.py:519
Async XLA Ops:
  0.0 36.5 %copy-start = (bf16[64,512]{1,0:T(8,128)(2,1)S(1)}, bf16[64,512]{1,0:T(8,128)(2,1)}, u32[]{:S(2)}) copy-start(bf16[64,512]{1,0:T(8,128)(2,1)} %param.19) | copy-start | bytes 196612

commit v4 on v3

--- a/solution.py
+++ b/solution.py
@@ -28,9 +28,9 @@
 
 
 def offsets(step):
-    i, j = step // X, lax.rem(step, X)
-    dz = Z // 2 + (1 - 2 * lax.rem(i, 2)) * ((i + 1) // 2)
-    dx = X // 2 + (1 - 2 * lax.rem(j, 2)) * ((j + 1) // 2)
+    i, j = step // X, step % X
+    dz = Z // 2 + (1 - 2 * (i % 2)) * ((i + 1) // 2)
+    dx = X // 2 + (1 - 2 * (j % 2)) * ((j + 1) // 2)
     return dz, dx
 
 
@@ -63,6 +63,7 @@
     table_ref,
     slot_ref,
     q_ref,
+    logits_ref,
     k_ref,
     v_ref,
     w_ref,
@@ -122,18 +123,18 @@
 
     barrier = pltpu.get_barrier_semaphore()
 
-    def greet_hosts(step, carry):
+    def greet_hosts(step):
         other = ahead_of(host, step)
         pl.semaphore_signal(barrier, inc=1, device_id=(other, lane), device_id_type=MESH)
-        return carry
-
-    def greet_lanes(step, carry):
+
+    def greet_lanes(step):
         other = lax.rem(lane + step, n_tp)
         pl.semaphore_signal(barrier, inc=1, device_id=(host, other), device_id_type=MESH)
-        return carry
-
-    lax.fori_loop(0, n_hst - 1, greet_hosts, 0)
-    lax.fori_loop(1, n_tp, greet_lanes, 0)
+
+    for step in range(n_hst - 1):
+        greet_hosts(step)
+    for step in range(1, n_tp):
+        greet_lanes(step)
 
     slots = table_ref.shape[1]
     row_total = slot_ref.shape[1]
@@ -170,50 +171,78 @@
     gather_lo = jnp.where(back_lane == back_place, 1.0, 0.0).astype(BF)
     gather_hi = jnp.where(back_lane == back_place + 8, 1.0, 0.0).astype(BF)
 
+    heads = q_ref.shape[1] // HD
+    tall = heads * 8
+    load_length.wait()
+    row = iota((row_total * heads, row_total), 0)
+    request = row // tall * 8 + lax.rem(row, 8)
+    length_col = jnp.sum(
+        jnp.where(iota(row.shape, 1) == request, length_ref[...], 0), axis=1, keepdims=True
+    )
+
     load_pages.wait()
-    load_length.wait()
     load_q.wait()
     load_k.wait()
     load_w.start()
     load_down.start()
     load_up.start()
-    load_v.wait()
-    heads = q_ref.shape[1] // HD
-    tall = heads * 16
-    member = lax.rem(iota((tall, HD), 0), 16)
-    token = iota((tall, HD), 1)
-    scale = 1.0 / math.sqrt(HD)
+    sub = iota((8, HD), 0)
 
     def pages_of(ref, row):
         return [ref[pages_ref[p, row]] for p in range(pages_ref.shape[0])]
 
-    def attend(group, carry):
-        first = pl.multiple_of(group * 16, 16)
-        q = q_ref[pl.ds(first, 16), :]
-        q = jnp.concatenate([q[:, j * HD : (j + 1) * HD] for j in range(heads)], axis=0)
-        logits = jnp.full((tall, HD), -jnp.inf, F32)
-        for r in range(0, 16, 2):
-            keys = jnp.concatenate(pages_of(k_ref, first + r) + pages_of(k_ref, first + r + 1), axis=0)
-            s = dot(q, keys, NT)
-            for i in range(2):
-                live = (member == r + i) & (token < length_ref[first + r + i])
-                logits = jnp.where(live, s[:, i * HD : (i + 1) * HD] * scale, logits)
-        top = jnp.max(logits, axis=1, keepdims=True)
-        e = jnp.exp(logits - top)
-        p = e / jnp.sum(e, axis=1, keepdims=True)
-        acc = jnp.zeros((tall, HD), F32)
-        for r in range(0, 16, 2):
-            values = jnp.concatenate(pages_of(v_ref, first + r) + pages_of(v_ref, first + r + 1), axis=0)
-            spread = jnp.concatenate([jnp.where(member == r + i, p, 0.0) for i in range(2)], axis=1)
-            acc = acc + dot(spread.astype(BF), values)
-        acc = acc.astype(BF)
-        for j in range(heads):
-            att_ref[pl.ds(first, 16), j * HD : (j + 1) * HD] = acc[j * 16 : (j + 1) * 16]
+    def pair_of(ref, row):
+        return jnp.concatenate(pages_of(ref, row) + pages_of(ref, row + 1), axis=0)
+
+    def match(step, carry):
+        first = pl.multiple_of(step * 16, 16)
+        q16 = q_ref[pl.ds(first, 16), :].astype(F32)
+        for part in range(2):
+            q = q16[part * 8 : (part + 1) * 8]
+            q = jnp.concatenate([q[:, j * HD : (j + 1) * HD] for j in range(heads)], axis=0).astype(BF)
+            got = [jnp.zeros((8, HD), F32)] * heads
+            for r in range(0, 8, 2):
+                s = dot(q, pair_of(k_ref, first + part * 8 + r), NT)
+                for j in range(heads):
+                    rows8 = s[j * 8 : (j + 1) * 8]
+                    got[j] = jnp.where(sub == r, rows8[:, :HD], got[j])
+                    got[j] = jnp.where(sub == r + 1, rows8[:, HD:], got[j])
+            logits_ref[pl.ds(pl.multiple_of((step * 2 + part) * tall, tall), tall), :] = jnp.concatenate(
+                got, axis=0
+            )
         return carry
 
-    lax.fori_loop(0, row_total // 16, attend, 0)
-
-    att = att_ref[...]
+    lax.fori_loop(0, row_total // 16, match, 0)
+
+    live = iota((row_total * heads, HD), 1) < length_col
+    logits = jnp.where(live, logits_ref[...] * (1.0 / math.sqrt(HD)), -jnp.inf)
+    e = jnp.exp(logits - jnp.max(logits, axis=1, keepdims=True))
+    logits_ref[...] = e / jnp.sum(e, axis=1, keepdims=True)
+
+    load_v.wait()
+
+    def blend(step, carry):
+        first = pl.multiple_of(step * 16, 16)
+        for part in range(2):
+            p = logits_ref[pl.ds(pl.multiple_of((step * 2 + part) * tall, tall), tall), :]
+            p = [p[j * 8 : (j + 1) * 8] for j in range(heads)]
+            acc = jnp.zeros((tall, HD), F32)
+            for r in range(0, 8, 2):
+                spread = jnp.concatenate(
+                    [
+                        jnp.concatenate([jnp.where(sub == r + i, x, 0.0) for x in p], axis=0)
+                        for i in range(2)
+                    ],
+                    axis=1,
+                )
+                acc = acc + dot(spread.astype(BF), pair_of(v_ref, first + part * 8 + r))
+            for j in range(heads):
+                att_ref[pl.ds(first + part * 8, 8), j * HD : (j + 1) * HD] = acc[j * 8 : (j + 1) * 8]
+        return carry
+
+    lax.fori_loop(0, row_total // 16, blend, 0)
+
+    att = att_ref[...].astype(BF)
     half = att.shape[1] // 2
 
     def pack(lo, hi):
@@ -225,19 +254,20 @@
     def unpack(x):
         rows = x.shape[0] * 8
         x = x.astype(F32)
-        return x[:, :8].reshape(rows, half).astype(BF), x[:, 8:].reshape(rows, half).astype(BF)
+        lo, hi = x[:, :8].reshape(rows, half), x[:, 8:].reshape(rows, half)
+        return jnp.concatenate([lo, hi], axis=1).astype(BF)
 
     rows_out[...] = pack(dot(scatter, att[:, :half]), dot(scatter, att[:, half:]))
 
     def arrived(ref, sem):
         pltpu.make_async_copy(ref, ref, sem).wait()
 
-    def table_copy(step):
+    def table_copy(step, group):
         return pltpu.make_async_remote_copy(
             src_ref=table_out.at[0:1, :],
-            dst_ref=tables.at[pl.ds(host, 1), :],
+            dst_ref=tables.at[pl.ds(step, 1), :],
             send_sem=table_send,
-            recv_sem=table_recv,
+            recv_sem=table_recv.at[group],
             device_id=(ahead_of(host, step), lane),
             device_id_type=MESH,
         )
@@ -257,16 +287,14 @@
     last = n_hst - 1
 
     pl.semaphore_wait(barrier, n_hst - 1 + n_tp - 1)
-    for group in range(GROUPS):
-
-        def send_rows(step, carry, group=group):
-            table_copy(step).start()
+    for group in reversed(range(GROUPS)):
+        first = group * group_hosts
+        for step in range(first, min(first + group_hosts, last)):
+            table_copy(step, group).start()
             rows_copy(step, group).start()
-            return carry
-
-        first = group * group_hosts
-        lax.fori_loop(first, min(first + group_hosts, last), send_rows, 0)
-    pltpu.make_async_copy(table_out.at[0:1, :], tables.at[pl.ds(host, 1), :], table_recv).start()
+    pltpu.make_async_copy(
+        table_out.at[0:1, :], tables.at[last : last + 1, :], table_recv.at[GROUPS - 1]
+    ).start()
     pltpu.make_async_copy(rows_out.at[host], rows_in.at[last], rows_recv.at[GROUPS - 1]).start()
 
     load_w.wait()
@@ -312,35 +340,28 @@
         base_copy(i).start()
     out_ref[...] = base_own[chips - 1] + pair_in[chips - 1].astype(F32)
 
-    arrived(tables, table_recv)
-    table = tables[...]
-    owned = jnp.right_shift(table, 5) == host
-    ahead = dot(
-        jnp.where(owned, 1.0, 0.0).astype(BF), jnp.where(s_sub < s_lane, 1.0, 0.0).astype(BF)
-    )
-    local_index = jnp.bitwise_and(table, 31).astype(F32)
-
-    def place_index(place):
-        got = jnp.where(owned & (ahead == place), local_index, -1.0)
-        return jnp.broadcast_to(jnp.max(got, axis=1, keepdims=True), got.shape).astype(BF)
-
     group_rows = group_hosts * 8
+    owned_total, rank, _ = down_ref.shape
     place_sub, place_lane = iota((group_rows, 128), 0), iota((group_rows, 128), 1)
+    from_host = iota((group_rows, group_hosts), 0) // 8 == iota((group_rows, group_hosts), 1)
+    from_host = jnp.where(from_host, 1.0, 0.0).astype(BF)
+    earlier = jnp.where(s_sub < s_lane, 1.0, 0.0).astype(BF)
 
     def adapters(group):
-        step = group * group_hosts + iota((group_rows, n_hst), 0) // 8
-        from_host = jnp.where(behind(host, step) == iota((group_rows, n_hst), 1), 1.0, 0.0).astype(BF)
-        return jnp.where(
-            lax.rem(place_sub, 8) < 4,
-            dot(from_host, place_index(0.0)),
-            dot(from_host, place_index(1.0)),
-        ) - jnp.where(place_lane >= 64, 1.0, 0.0)
-
-    adapter = [adapters(group) for group in range(GROUPS)]
-
-    owned_total, rank, _ = down_ref.shape
-    both = group_rows // 2
-    low_half = iota((both, 128), 1) < 64
+        first = group * group_hosts
+        table = tables[first : first + group_hosts]
+        owned = jnp.right_shift(table, 5) == host
+        ahead = dot(jnp.where(owned, 1.0, 0.0).astype(BF), earlier)
+        local_index = jnp.bitwise_and(table, 31).astype(F32)
+
+        def place_index(place):
+            got = jnp.where(owned & (ahead == place), local_index, -1.0)
+            got = jnp.broadcast_to(jnp.max(got, axis=1, keepdims=True), got.shape).astype(BF)
+            return dot(from_host, got)
+
+        found = jnp.where(lax.rem(place_sub, 8) < 4, place_index(0.0), place_index(1.0))
+        return found - jnp.where(place_lane >= 64, 1.0, 0.0), found.T[:rank]
+
 
     def part_copy(group, step):
         return pltpu.make_async_remote_copy(
@@ -353,27 +374,24 @@
         )
 
     load_down.wait()
-    own_part = []
-    for group in range(GROUPS):
+    own_part, adapter = {}, {}
+    for group in reversed(range(GROUPS)):
         first = group * group_hosts
+        arrived(tables.at[first : first + group_hosts], table_recv.at[group])
+        adapter[group], adapter_lane = adapters(group)
         arrived(rows_in.at[first : first + group_hosts], rows_recv.at[group])
-        x_lo, x_hi = unpack(rows_in[first : first + group_hosts])
-        folded = jnp.zeros((group_rows, 128), F32)
+        x = unpack(rows_in[first : first + group_hosts])
+        folded = jnp.zeros((rank, group_rows), F32)
         for c in range(0, owned_total, 4):
-            d = down_ref[c : c + 4].reshape(4 * rank, 2 * half)
-            s = dot(x_lo, d[:, :half], NT) + dot(x_hi, d[:, half:], NT)
-            folded = folded + jnp.where(adapter[group] == float(c), s[:, :128], 0.0)
-            folded = folded + jnp.where(adapter[group] == float(c + 2), s[:, 128:], 0.0)
-        folded = folded + pltpu.roll(folded, 64, 1)
-        part = jnp.where(low_half, folded[:both], folded[both:])
-        own_part.append(part)
-        part_out[group] = part.astype(BF)
-
-        def send_part(step, carry, group=group):
+            s = dot(down_ref[c : c + 4].reshape(4 * rank, 2 * half), x, NT)
+            for i in range(4):
+                folded = folded + jnp.where(
+                    adapter_lane == float(c + i), s[i * rank : (i + 1) * rank], 0.0
+                )
+        own_part[group] = folded
+        part_out[group] = folded.astype(BF)
+        for step in (4, 5, 3, 2, 6, 7, 1):
             part_copy(group, step).start()
-            return carry
-
-        lax.fori_loop(1, n_tp, send_part, 0)
 
     arrived(base_in, base_recv)
     base = out_ref[...]
@@ -392,20 +410,13 @@
             device_id_type=MESH,
         )
 
-    def send_back(step, carry):
-        back_copy(step).start()
-        return carry
-
     load_up.wait()
-    for group in range(GROUPS):
+    for group in reversed(range(GROUPS)):
         arrived(part_in.at[group], part_recv.at[group])
         g = own_part[group]
         for step in range(1, n_tp):
             g = g + part_in[group, step - 1].astype(F32)
-        turned = pltpu.roll(g, 64, 1)
-        full = jnp.concatenate(
-            [jnp.where(low_half, g, turned), jnp.where(low_half, turned, g)], axis=0
-        )
+        full = jnp.concatenate([g, g], axis=0).T
         raised = jnp.zeros((group_rows, 2 * half), F32)
         for c in range(0, owned_total, 4):
             e = jnp.concatenate(
@@ -418,7 +429,8 @@
             raised = raised + dot(e, up_ref[c : c + 4].reshape(4 * rank, 2 * half))
         first = group * group_hosts
         back_out[first : first + group_hosts] = pack(raised[:, :half], raised[:, half:])
-        lax.fori_loop(first, min(first + group_hosts, last), send_back, 0)
+        for step in range(first, min(first + group_hosts, last)):
+            back_copy(step).start()
 
     pltpu.make_async_copy(back_out.at[last], back_in.at[host], back_recv).start()
     arrived(back_in, back_recv)
@@ -457,7 +469,7 @@
         key_page_cache,
         value_page_cache,
         request_pages.T,
-        context_length,
+        context_length.reshape(1, -1),
         output_weight,
         adapter_down_weight,
         adapter_up_weight,
@@ -471,16 +483,17 @@
         out_specs=pl.BlockSpec(memory_space=pltpu.VMEM),
         scratch_shapes=[
             pltpu.SMEM(request_pages.shape[::-1], jnp.int32),
-            pltpu.SMEM(context_length.shape, jnp.int32),
+            pltpu.VMEM((1, rows), jnp.int32),
             pltpu.VMEM((1, host_slot_adapter.shape[0]), jnp.int32),
             pltpu.VMEM((1, rows), jnp.int32),
             pltpu.VMEM(queries.shape, BF),
+            pltpu.VMEM((rows * width // HD, HD), F32),
             pltpu.VMEM(key_page_cache.shape, BF),
             pltpu.VMEM(value_page_cache.shape, BF),
             pltpu.VMEM(output_weight.shape, BF),
             pltpu.VMEM(adapter_down_weight.shape, BF),
             pltpu.VMEM(adapter_up_weight.shape, BF),
-            pltpu.VMEM(queries.shape, BF),
+            pltpu.VMEM(queries.shape, F32),
             pltpu.VMEM((8, 128), jnp.int32),
             pltpu.VMEM((n_hst, 128), jnp.int32),
             pltpu.VMEM(block, BF),
@@ -496,7 +509,7 @@
             pltpu.VMEM((GROUPS, n_tp - 1, part_rows, 128), BF),
             dma((10,)),
             dma,
-            dma,
+            dma((GROUPS,)),
             dma,
             dma((GROUPS,)),
             dma,

time: 37.2 us -> 34.8 us (0.935)
  Pallas kernels: 36.5 us -> 34.1 us
    pallas_call x1, Pallas kernels: 36.5 us -> 34.1 us  [local(): pl.pallas_call(functools.partial(kernel, n_hst, n_tp), out_shape=jax.Shap...]
where the time goes in v4:
time: 34.8 us; the launch traced here: 34.7 us
  Pallas kernels  34.1 us (98%)
  other arithmetic  0.64 us (2%)
    pallas_call x1, Pallas kernels, local(): pl.pallas_call(functools.partial(kernel, n_hst, n_tp), out_shape=jax.Shap...  34.1 us

profile of v4, /device:TPU:1, one launch (start us, length us, event | category | flops | bytes accessed | tf_op | source)
XLA Modules:
  0.0 34.7 jit_solution(9242569407779871174)
XLA Ops:
  0.0 0.0 copy-start
  0.0 34.1 %decode_step.1 = f32[64,512]{1,0:T(8,128)S(1)} custom-call(bf16[64,512]{1,0:T(8,128)(2,1)} %q_hbm.1, bf16[512,16,128]{2,1,0:T(8,128)(2,1)} %k_hbm.1, bf16[512,16,128]{2,1,0:T(8,128)(2,1)} %v_hbm.1, s32[8,64]{1,0:T(8,128)} %bitcast.4, s32[1,64]{1,0:T(1,128)} %bitcast.5, bf16[512,4096]{1,0:T(8,128)(2,1)} %w_hbm.1, bf16[32,64,512]{2,1,0:T(8,128)(2,1)} %down_hbm.1, ...), custom_call_target="tpu_custom_call" | custom-call | flops 2000000000 | bytes 12000000 | tf_op jit(solution)/shard_map/decode_step/pallas_call | solution.py:479
  34.1 0.0 copy-done
  34.1 0.6 %add_convert_fusion = bf16[64,512]{1,0:T(8,128)(2,1)} fusion(f32[64,512]{1,0:T(8,128)S(1)} %decode_step.1, bf16[64,512]{1,0:T(8,128)(2,1)S(1)} %copy-done), kind=kLoop, calls=%fused_computation | loop fusion | flops 98304 | bytes 262144 | tf_op jit(solution)/shard_map/convert_element_type | solution.py:532
Async XLA Ops:
  0.0 34.1 %copy-start = (bf16[64,512]{1,0:T(8,128)(2,1)S(1)}, bf16[64,512]{1,0:T(8,128)(2,1)}, u32[]{:S(2)}) copy-start(bf16[64,512]{1,0:T(8,128)(2,1)} %param.19) | copy-start | bytes 196612

commit v5 on v4

--- a/solution.py
+++ b/solution.py
@@ -11,7 +11,7 @@
 HD = 128
 ADAPTER_SCALE = 2.0
 Z, X = 8, 4
-GROUPS = 2
+GROUPS = 4
 MESH = pl.DeviceIdType.MESH
 BF = jnp.bfloat16
 F32 = jnp.float32
@@ -28,10 +28,9 @@
 
 
 def offsets(step):
-    i, j = step // X, step % X
-    dz = Z // 2 + (1 - 2 * (i % 2)) * ((i + 1) // 2)
-    dx = X // 2 + (1 - 2 * (j % 2)) * ((j + 1) // 2)
-    return dz, dx
+    i, j = step // Z, step % Z
+    dz = Z // 2 + (1 - 2 * (j % 2)) * ((j + 1) // 2)
+    return dz, (2, 3, 1, 0)[i]
 
 
 def ahead_of(host, step):
@@ -150,7 +149,11 @@
     place_row = jnp.sum(
         jnp.where((owner_col == owner_all) & (s_sub < s_lane), 1, 0), axis=0, keepdims=True
     )
-    start_row = owner_row * 8 + place_row * 4
+    dz = jnp.bitwise_and(jnp.right_shift(owner_row, 2) - host // X + Z, Z - 1)
+    dx = jnp.bitwise_and(jnp.bitwise_and(owner_row, X - 1) - lax.rem(host, X) + X, X - 1)
+    z_order = jnp.where(dz >= Z // 2, 2 * dz - Z, Z - 1 - 2 * dz)
+    x_order = jnp.where(dx >= X // 2, dx - X // 2, X - 1 - dx)
+    start_row = (x_order * Z + z_order) * 8 + place_row * 4
     chosen_row = slot_ref[...]
     r_sub, r_lane = iota((row_total, 128), 0), iota((row_total, 128), 1)
     q_sub, q_lane = iota((row_total, row_total), 0), iota((row_total, row_total), 1)
@@ -257,7 +260,6 @@
         lo, hi = x[:, :8].reshape(rows, half), x[:, 8:].reshape(rows, half)
         return jnp.concatenate([lo, hi], axis=1).astype(BF)
 
-    rows_out[...] = pack(dot(scatter, att[:, :half]), dot(scatter, att[:, half:]))
 
     def arrived(ref, sem):
         pltpu.make_async_copy(ref, ref, sem).wait()
@@ -273,13 +275,12 @@
         )
 
     def rows_copy(step, group):
-        other = ahead_of(host, step)
         return pltpu.make_async_remote_copy(
-            src_ref=rows_out.at[other],
+            src_ref=rows_out.at[step],
             dst_ref=rows_in.at[step],
             send_sem=rows_send,
             recv_sem=rows_recv.at[group],
-            device_id=(other, lane),
+            device_id=(ahead_of(host, step), lane),
             device_id_type=MESH,
         )
 
@@ -287,15 +288,17 @@
     last = n_hst - 1
 
     pl.semaphore_wait(barrier, n_hst - 1 + n_tp - 1)
-    for group in reversed(range(GROUPS)):
+    for group in range(GROUPS):
         first = group * group_hosts
+        spread = dot(scatter[first * 8 : (first + group_hosts) * 8], att)
+        rows_out[first : first + group_hosts] = pack(spread[:, :half], spread[:, half:])
         for step in range(first, min(first + group_hosts, last)):
             table_copy(step, group).start()
             rows_copy(step, group).start()
     pltpu.make_async_copy(
         table_out.at[0:1, :], tables.at[last : last + 1, :], table_recv.at[GROUPS - 1]
     ).start()
-    pltpu.make_async_copy(rows_out.at[host], rows_in.at[last], rows_recv.at[GROUPS - 1]).start()
+    pltpu.make_async_copy(rows_out.at[last], rows_in.at[last], rows_recv.at[GROUPS - 1]).start()
 
     load_w.wait()
     width = out_ref.shape[1]
@@ -375,7 +378,7 @@
 
     load_down.wait()
     own_part, adapter = {}, {}
-    for group in reversed(range(GROUPS)):
+    for group in range(GROUPS):
         first = group * group_hosts
         arrived(tables.at[first : first + group_hosts], table_recv.at[group])
         adapter[group], adapter_lane = adapters(group)
@@ -389,7 +392,7 @@
                     adapter_lane == float(c + i), s[i * rank : (i + 1) * rank], 0.0
                 )
         own_part[group] = folded
-        part_out[group] = folded.astype(BF)
+        part_out[group] = jnp.concatenate([folded[: rank // 2], folded[rank // 2 :]], axis=1).astype(BF)
         for step in (4, 5, 3, 2, 6, 7, 1):
             part_copy(group, step).start()
 
@@ -399,23 +402,24 @@
         base = base + base_in[i].astype(F32)
     out_ref[...] = base
 
-    def back_copy(step):
+    def back_copy(step, group):
         other = behind(host, step)
         return pltpu.make_async_remote_copy(
             src_ref=back_out.at[step],
-            dst_ref=back_in.at[host],
+            dst_ref=back_in.at[step],
             send_sem=back_send,
-            recv_sem=back_recv,
+            recv_sem=back_recv.at[group],
             device_id=(other, lane),
             device_id_type=MESH,
         )
 
     load_up.wait()
-    for group in reversed(range(GROUPS)):
+    for group in range(GROUPS):
         arrived(part_in.at[group], part_recv.at[group])
-        g = own_part[group]
-        for step in range(1, n_tp):
+        g = part_in[group, 0].astype(F32)
+        for step in range(2, n_tp):
             g = g + part_in[group, step - 1].astype(F32)
+        g = own_part[group] + jnp.concatenate([g[:, :group_rows], g[:, group_rows:]], axis=0)
         full = jnp.concatenate([g, g], axis=0).T
         raised = jnp.zeros((group_rows, 2 * half), F32)
         for c in range(0, owned_total, 4):
@@ -430,13 +434,19 @@
         first = group * group_hosts
         back_out[first : first + group_hosts] = pack(raised[:, :half], raised[:, half:])
         for step in range(first, min(first + group_hosts, last)):
-            back_copy(step).start()
-
-    pltpu.make_async_copy(back_out.at[last], back_in.at[host], back_recv).start()
-    arrived(back_in, back_recv)
-    y = back_in[...].reshape(n_hst * 16, half)
-    out_ref[:, :half] += ADAPTER_SCALE * dot(gather_lo, y)
-    out_ref[:, half:] += ADAPTER_SCALE * dot(gather_hi, y)
+            back_copy(step, group).start()
+
+    pltpu.make_async_copy(back_out.at[last], back_in.at[last], back_recv.at[GROUPS - 1]).start()
+    given_lo, given_hi = 0.0, 0.0
+    for group in range(GROUPS):
+        first = group * group_hosts
+        arrived(back_in.at[first : first + group_hosts], back_recv.at[group])
+        y = back_in[first : first + group_hosts].reshape(group_hosts * 16, half)
+        mine = slice(first * 16, (first + group_hosts) * 16)
+        given_lo = given_lo + dot(gather_lo[:, mine], y)
+        given_hi = given_hi + dot(gather_hi[:, mine], y)
+    out_ref[:, :half] += ADAPTER_SCALE * given_lo
+    out_ref[:, half:] += ADAPTER_SCALE * given_hi
 
     arrived(tables.at[0:last], table_send)
     arrived(rows_out.at[0:last], rows_send)
@@ -513,7 +523,7 @@
             dma,
             dma((GROUPS,)),
             dma,
-            dma,
+            dma((GROUPS,)),
             dma,
             dma,
             dma,

time: 34.8 us -> 32.5 us (0.934)
  Pallas kernels: 34.1 us -> 31.8 us
    pallas_call x1, Pallas kernels: 34.1 us -> 31.8 us  [local(): pl.pallas_call(functools.partial(kernel, n_hst, n_tp), out_shape=jax.Shap...]
where the time goes in v5:
time: 32.5 us
  Pallas kernels  31.8 us (98%)
  other arithmetic  0.64 us (2%)
    pallas_call x1, Pallas kernels, local(): pl.pallas_call(functools.partial(kernel, n_hst, n_tp), out_shape=jax.Shap...  31.8 us

profile of v5, /device:TPU:1, one launch (start us, length us, event | category | flops | bytes accessed | tf_op | source)
XLA Modules:
  0.0 32.5 jit_solution(4736927031405190896)
XLA Ops:
  0.0 0.0 copy-start
  0.0 31.8 %decode_step.1 = f32[64,512]{1,0:T(8,128)S(1)} custom-call(bf16[64,512]{1,0:T(8,128)(2,1)} %q_hbm.1, bf16[512,16,128]{2,1,0:T(8,128)(2,1)} %k_hbm.1, bf16[512,16,128]{2,1,0:T(8,128)(2,1)} %v_hbm.1, s32[8,64]{1,0:T(8,128)} %bitcast.4, s32[1,64]{1,0:T(1,128)} %bitcast.5, bf16[512,4096]{1,0:T(8,128)(2,1)} %w_hbm.1, bf16[32,64,512]{2,1,0:T(8,128)(2,1)} %down_hbm.1, ...), custom_call_target="tpu_custom_call" | custom-call | flops 2000000000 | bytes 12000000 | tf_op jit(solution)/shard_map/decode_step/pallas_call | solution.py:489
  31.8 0.0 copy-done
  31.8 0.6 %add_convert_fusion = bf16[64,512]{1,0:T(8,128)(2,1)} fusion(f32[64,512]{1,0:T(8,128)S(1)} %decode_step.1, bf16[64,512]{1,0:T(8,128)(2,1)S(1)} %copy-done), kind=kLoop, calls=%fused_computation | loop fusion | flops 98304 | bytes 262144 | tf_op jit(solution)/shard_map/convert_element_type | solution.py:542
Async XLA Ops:
  0.0 31.8 %copy-start = (bf16[64,512]{1,0:T(8,128)(2,1)S(1)}, bf16[64,512]{1,0:T(8,128)(2,1)}, u32[]{:S(2)}) copy-start(bf16[64,512]{1,0:T(8,128)(2,1)} %param.19) | copy-start | bytes 196612

commit v6 on v5

--- a/solution.py
+++ b/solution.py
@@ -421,16 +421,10 @@
             g = g + part_in[group, step - 1].astype(F32)
         g = own_part[group] + jnp.concatenate([g[:, :group_rows], g[:, group_rows:]], axis=0)
         full = jnp.concatenate([g, g], axis=0).T
-        raised = jnp.zeros((group_rows, 2 * half), F32)
-        for c in range(0, owned_total, 4):
-            e = jnp.concatenate(
-                [
-                    jnp.where(adapter[group] == float(c), full, 0.0),
-                    jnp.where(adapter[group] == float(c + 2), full, 0.0),
-                ],
-                axis=1,
-            ).astype(BF)
-            raised = raised + dot(e, up_ref[c : c + 4].reshape(4 * rank, 2 * half))
+        spread_up = jnp.concatenate(
+            [jnp.where(adapter[group] == float(c), full, 0.0) for c in range(0, owned_total, 2)], axis=1
+        )
+        raised = dot(spread_up.astype(BF), up_ref[...].reshape(owned_total * rank, 2 * half))
         first = group * group_hosts
         back_out[first : first + group_hosts] = pack(raised[:, :half], raised[:, half:])
         for step in range(first, min(first + group_hosts, last)):

time: 32.5 us -> 32.5 us (level)
  no operation moved by 1% of the time
where the time goes in v6:
time: 32.5 us
  Pallas kernels  31.8 us (98%)
  other arithmetic  0.64 us (2%)
    pallas_call x1, Pallas kernels, local(): pl.pallas_call(functools.partial(kernel, n_hst, n_tp), out_shape=jax.Shap...  31.8 us

profile of v6, /device:TPU:1, one launch (start us, length us, event | category | flops | bytes accessed | tf_op | source)
XLA Modules:
  0.0 32.5 jit_solution(1363012969732547744)
XLA Ops:
  0.0 0.0 copy-start
  0.0 31.8 %decode_step.1 = f32[64,512]{1,0:T(8,128)S(1)} custom-call(bf16[64,512]{1,0:T(8,128)(2,1)} %q_hbm.1, bf16[512,16,128]{2,1,0:T(8,128)(2,1)} %k_hbm.1, bf16[512,16,128]{2,1,0:T(8,128)(2,1)} %v_hbm.1, s32[8,64]{1,0:T(8,128)} %bitcast.4, s32[1,64]{1,0:T(1,128)} %bitcast.5, bf16[512,4096]{1,0:T(8,128)(2,1)} %w_hbm.1, bf16[32,64,512]{2,1,0:T(8,128)(2,1)} %down_hbm.1, ...), custom_call_target="tpu_custom_call" | custom-call | flops 2000000000 | bytes 12000000 | tf_op jit(solution)/shard_map/decode_step/pallas_call | solution.py:483
  31.8 0.0 copy-done
  31.8 0.6 %add_convert_fusion = bf16[64,512]{1,0:T(8,128)(2,1)} fusion(f32[64,512]{1,0:T(8,128)S(1)} %decode_step.1, bf16[64,512]{1,0:T(8,128)(2,1)S(1)} %copy-done), kind=kLoop, calls=%fused_computation | loop fusion | flops 98304 | bytes 262144 | tf_op jit(solution)/shard_map/convert_element_type | solution.py:536
Async XLA Ops:
  0.0 31.8 %copy-start = (bf16[64,512]{1,0:T(8,128)(2,1)S(1)}, bf16[64,512]{1,0:T(8,128)(2,1)}, u32[]{:S(2)}) copy-start(bf16[64,512]{1,0:T(8,128)(2,1)} %param.19) | copy-start | bytes 196612

commit v7 on v6

--- a/solution.py
+++ b/solution.py
@@ -385,9 +385,9 @@
         arrived(rows_in.at[first : first + group_hosts], rows_recv.at[group])
         x = unpack(rows_in[first : first + group_hosts])
         folded = jnp.zeros((rank, group_rows), F32)
-        for c in range(0, owned_total, 4):
-            s = dot(down_ref[c : c + 4].reshape(4 * rank, 2 * half), x, NT)
-            for i in range(4):
+        for c in range(0, owned_total, 2):
+            s = dot(down_ref[c : c + 2].reshape(2 * rank, 2 * half), x, NT)
+            for i in range(2):
                 folded = folded + jnp.where(
                     adapter_lane == float(c + i), s[i * rank : (i + 1) * rank], 0.0
                 )

time: 32.5 us -> 32.5 us (level)
  no operation moved by 1% of the time
where the time goes in v7:
time: 32.5 us
  Pallas kernels  31.8 us (98%)
  other arithmetic  0.64 us (2%)
    pallas_call x1, Pallas kernels, local(): pl.pallas_call(functools.partial(kernel, n_hst, n_tp), out_shape=jax.Shap...  31.8 us

profile of v7, /device:TPU:1, one launch (start us, length us, event | category | flops | bytes accessed | tf_op | source)
XLA Modules:
  0.0 32.5 jit_solution(16597735996131339819)
XLA Ops:
  0.0 0.0 copy-start
  0.0 31.8 %decode_step.1 = f32[64,512]{1,0:T(8,128)S(1)} custom-call(bf16[64,512]{1,0:T(8,128)(2,1)} %q_hbm.1, bf16[512,16,128]{2,1,0:T(8,128)(2,1)} %k_hbm.1, bf16[512,16,128]{2,1,0:T(8,128)(2,1)} %v_hbm.1, s32[8,64]{1,0:T(8,128)} %bitcast.4, s32[1,64]{1,0:T(1,128)} %bitcast.5, bf16[512,4096]{1,0:T(8,128)(2,1)} %w_hbm.1, bf16[32,64,512]{2,1,0:T(8,128)(2,1)} %down_hbm.1, ...), custom_call_target="tpu_custom_call" | custom-call | flops 2000000000 | bytes 12000000 | tf_op jit(solution)/shard_map/decode_step/pallas_call | solution.py:483
  31.8 0.0 copy-done
  31.8 0.6 %add_convert_fusion = bf16[64,512]{1,0:T(8,128)(2,1)} fusion(f32[64,512]{1,0:T(8,128)S(1)} %decode_step.1, bf16[64,512]{1,0:T(8,128)(2,1)S(1)} %copy-done), kind=kLoop, calls=%fused_computation | loop fusion | flops 98304 | bytes 262144 | tf_op jit(solution)/shard_map/convert_element_type | solution.py:536
Async XLA Ops:
  0.0 31.8 %copy-start = (bf16[64,512]{1,0:T(8,128)(2,1)S(1)}, bf16[64,512]{1,0:T(8,128)(2,1)}, u32[]{:S(2)}) copy-start(bf16[64,512]{1,0:T(8,128)(2,1)} %param.19) | copy-start | bytes 196612
